TPU v7x, 512 devices: a whole 4x4x16 slice. The times are simulated.
512 devices in a mesh: ctx: 64 (over y, z), tp: 8 (over x, core).
Axes of the slice: x: 4, y: 4, z: 16, core: 2. Of those that a mesh axis runs over, the one named last changes fastest.
Arguments:
- lin_query: bfloat16 [8192, 4096], P('ctx', 'tp'), may hold values from -6 to 6
- lin_key: bfloat16 [8192, 4096], P('ctx', 'tp'), may hold values from -6 to 6
- lin_value: bfloat16 [8192, 4096], P('ctx', 'tp'), may hold values from -6 to 6
- lin_cotangent: bfloat16 [8192, 4096], P('ctx', 'tp'), may hold values from -6 to 6
- soft_query: bfloat16 [8192, 4096], P('ctx', 'tp'), may hold values from -200 to 200
- soft_key: bfloat16 [8192, 1024], P('ctx', 'tp'), may hold values from -200 to 200
- soft_value: bfloat16 [8192, 1024], P('ctx', 'tp'), may hold values from -6 to 6
- doc_start: int32 [8192], P('ctx'), may hold values from 0 to 8191, as said below
Outputs:
- lin_out: bfloat16 [8192, 4096], P('ctx', 'tp')
- grad_query: bfloat16 [8192, 4096], P('ctx', 'tp')
- grad_key: bfloat16 [8192, 4096], P('ctx', 'tp')
- grad_value: bfloat16 [8192, 4096], P('ctx', 'tp')
- soft_out: bfloat16 [8192, 4096], P('ctx', 'tp')
Inputs may be any that keep to these rules, and one draw needn't show every extreme that they name: doc_start[i] <= i, doc_start never falls along the sequence, doc_start[0] = 0, doc_start[i] equals i or doc_start[i - 1], and a document of one position starts at position 8191.
All inputs are finite; a program needn't handle non-finite values.
Results may differ from a plain program's by a relative error of at most 0.011.
Values may be sent and summed in bfloat16 or wider, within the bound.
No kernel may reach another device: no remote copies, remote signals or barrier semaphores. Data moves between devices by JAX's collectives and lax.ppermute only.
A program may use at most 128 MiB of HBM per device.

v0:
```python
import math

import jax
import jax.numpy as jnp
from jax import lax
from jax.sharding import PartitionSpec as P

HD = 128
LH = 32
SH = 32
KVH = 8


epsilon = 1e-06
highest = lax.Precision.HIGHEST
floor_score = -1e30


def carried_in(value, axis, combine, identity, reverse):
    length, position = (lax.axis_size(axis), lax.axis_index(axis))
    everything = lax.all_gather(value.astype(jnp.bfloat16), axis)
    start = jnp.broadcast_to(jnp.asarray(identity, value.dtype), value.shape)

    def hop(k, before):
        at = length - 1 - k if reverse else k
        reached = at > position if reverse else at < position
        new = combine(before, everything[at].astype(value.dtype))
        return jnp.where(reached, new, before)

    return lax.fori_loop(0, length, hop, start)


def on_device(
    lin_query, lin_key, lin_value, lin_cotangent, soft_query, soft_key, soft_value, doc_start
):
    length = lin_query.shape[0]
    heads_here = lin_query.shape[1] // HD
    queries = lin_query.reshape(length, heads_here, HD)
    keys = lin_key.reshape(length, heads_here, HD)
    values = lin_value.reshape(length, heads_here, HD)
    lower = jnp.tril(jnp.ones((length, length), dtype=bool))
    raw_scores = jnp.einsum("thd,shd->hts", queries, keys, preferred_element_type=jnp.float32)
    weights = jnp.where(lower[None], raw_scores, 0.0).astype(jnp.bfloat16)
    own_state = jnp.einsum("thd,the->hde", keys, values, preferred_element_type=jnp.float32)
    earlier = carried_in(own_state, "ctx", jnp.add, jnp.zeros_like(own_state), False)
    mixed = jnp.einsum("hts,shd->thd", weights, values, preferred_element_type=jnp.float32)
    mixed = mixed + jnp.einsum(
        "thd,hde->the", queries.astype(jnp.float32), earlier, precision=highest
    )
    mixed = mixed.reshape(length, heads_here * HD)
    squares = lax.psum(jnp.sum(mixed * mixed, axis=1), "tp")
    scale = lax.rsqrt(squares / (LH * HD) + epsilon)
    normed = mixed * scale[:, None]
    lin_out = normed.astype(jnp.bfloat16)
    grad = lin_cotangent.astype(jnp.float32)
    inner = lax.psum(jnp.sum(grad * normed, axis=1), "tp")
    grad_mix = scale[:, None] * (grad - normed * (inner / (LH * HD))[:, None])
    grad_mix = grad_mix.astype(jnp.bfloat16).reshape(length, heads_here, HD)
    own_adjoint = jnp.einsum("thd,the->hde", queries, grad_mix, preferred_element_type=jnp.float32)
    later = carried_in(own_adjoint, "ctx", jnp.add, jnp.zeros_like(own_adjoint), True)
    raw_grad = jnp.einsum("the,she->hts", grad_mix, values, preferred_element_type=jnp.float32)
    grad_scores = jnp.where(lower[None], raw_grad, 0.0).astype(jnp.bfloat16)
    grad_q = jnp.einsum("hts,shd->thd", grad_scores, keys, preferred_element_type=jnp.float32)
    grad_q = grad_q + jnp.einsum(
        "the,hde->thd", grad_mix.astype(jnp.float32), earlier, precision=highest
    )
    grad_k = jnp.einsum("hts,thd->shd", grad_scores, queries, preferred_element_type=jnp.float32)
    grad_k = grad_k + jnp.einsum(
        "she,hde->shd", values.astype(jnp.float32), later, precision=highest
    )
    grad_v = jnp.einsum("hts,thd->shd", weights, grad_mix, preferred_element_type=jnp.float32)
    grad_v = grad_v + jnp.einsum("shd,hde->she", keys.astype(jnp.float32), later, precision=highest)
    grad_query = grad_q.reshape(length, heads_here * HD).astype(jnp.bfloat16)
    grad_key = grad_k.reshape(length, heads_here * HD).astype(jnp.bfloat16)
    grad_value = grad_v.reshape(length, heads_here * HD).astype(jnp.bfloat16)
    group = SH // KVH
    kv_here = soft_key.shape[1] // HD
    factor = 1.0 / math.sqrt(HD)
    soft_q = soft_query.reshape(length, kv_here, group, HD)
    my_first = lax.axis_index("ctx") * length
    query_pos = my_first + jnp.arange(length, dtype=jnp.int32)

    def attend(carry, key_rows, value_rows, start):
        count = key_rows.shape[0]
        key_pos = start + jnp.arange(count, dtype=jnp.int32)
        allowed = (key_pos[None, :] <= query_pos[:, None]) & (
            key_pos[None, :] >= doc_start[:, None]
        )
        key_heads = key_rows.reshape(count, kv_here, HD)
        value_heads = value_rows.reshape(count, kv_here, HD)
        scores = (
            jnp.einsum("tkgd,nkd->kgtn", soft_q, key_heads, preferred_element_type=jnp.float32)
            * factor
        )
        scores = jnp.where(allowed, scores, floor_score)
        old_top, old_total, old_acc = carry
        new_top = jnp.maximum(old_top, jnp.max(scores, axis=-1))
        probs = jnp.where(allowed, jnp.exp(scores - new_top[..., None]), 0.0)
        shrink = jnp.exp(old_top - new_top)
        new_total = shrink * old_total + jnp.sum(probs, axis=-1)
        update = jnp.einsum(
            "kgtn,nkd->kgtd",
            probs.astype(jnp.bfloat16),
            value_heads,
            preferred_element_type=jnp.float32,
        )
        return (new_top, new_total, shrink[..., None] * old_acc + update)

    def visit(carry, key_rows, value_rows, start):
        return attend(carry, key_rows, value_rows, start)

    initial = (
        jnp.full((kv_here, group, length), floor_score, jnp.float32),
        jnp.zeros((kv_here, group, length), jnp.float32),
        jnp.zeros((kv_here, group, length, HD), jnp.float32),
    )
    key_rows = lax.all_gather(soft_key, "ctx", axis=0, tiled=True)
    value_rows = lax.all_gather(soft_value, "ctx", axis=0, tiled=True)
    count = key_rows.shape[0]
    block = math.gcd(count, 512)

    def inner_step(index, state):
        key_part = lax.dynamic_slice_in_dim(key_rows, index * block, block, 0)
        value_part = lax.dynamic_slice_in_dim(value_rows, index * block, block, 0)
        return visit(state, key_part, value_part, index * block)

    final = lax.fori_loop(0, count // block, inner_step, initial)
    top, total, accum = final
    result = accum / total[..., None]
    soft_out = (
        jnp.transpose(result, (2, 0, 1, 3))
        .reshape(length, kv_here * group * HD)
        .astype(jnp.bfloat16)
    )
    return (lin_out, grad_query, grad_key, grad_value, soft_out)


def solution(mesh):
    placed = (
        P("ctx", "tp"),
        P("ctx", "tp"),
        P("ctx", "tp"),
        P("ctx", "tp"),
        P("ctx", "tp"),
        P("ctx", "tp"),
        P("ctx", "tp"),
        P("ctx"),
    )
    return jax.shard_map(
        on_device,
        mesh=mesh,
        in_specs=placed,
        out_specs=(P("ctx", "tp"), P("ctx", "tp"), P("ctx", "tp"), P("ctx", "tp"), P("ctx", "tp")),
        check_vma=False,
    )
```

profile of v0, /device:TPU:24, one launch (start us, length us, event | category | flops | bytes accessed | tf_op | source)
XLA Modules:
  0.0 683.0 jit_solution(14521103591499810169)
XLA Ops:
  7.2 1.1 copy.141
  8.3 1.7 convolution_convert_fusion.1
  11.7 1.1 fusion.24
  12.8 1.1 convolution_bitcast_fusion.6
  15.1 155.6 %all-gather.11.cloned.1.call-done = bf16[256,128,128]{2,1,0:T(8,128)(2,1)} async-done(((bf16[4,128,128]{2,1,0:T(8,128)(2,1)}), bf16[256,128,128]{2,1,0:T(8,128)(2,1)}) %all-gather.11.cloned.1.call-update) | async-done | bytes 8388624 | tf_op jit(solution)/shard_map/all_gather | solution.py:21
  170.7 67.9 %while.48 = (s32[]{:T(128)}, f32[4,128,128]{2,1,0:T(8,128)S(1)}, s32[]{:T(128)}, bf16[64,4,128,128]{3,2,1,0:T(8,128)(2,1)}, s32[]{:T(128)}, /*index=5*/s32[]{:T(128)}) while((s32[]{:T(128)}, f32[4,128,128]{2,1,0:T(8,128)S(1)}, s32[]{:T(128)}, bf16[64,4,128,128]{3,2,1,0:T(8,128)(2,1)}, s32[]{:T(128)}, /*index=5*/s32[]{:T(128)}) %tuple.131), condition=%wide.region_1.2_spmd.clone, body=%wide.region_0.1_spmd.clone.sunk | while | flops 262148 | bytes 655453 | solution.py:30
  170.7 1.1 add_select_fusion.4
  171.8 1.0 add_select_fusion.4
  173.9 1.0 add_select_fusion.4
  175.0 1.0 add_select_fusion.4
  177.1 1.0 add_select_fusion.4
  178.2 1.0 add_select_fusion.4
  180.3 1.0 add_select_fusion.4
  181.4 1.0 add_select_fusion.4
  183.5 1.0 add_select_fusion.4
  184.5 1.0 add_select_fusion.4
  185.6 1.0 add_select_fusion.4
  186.7 1.0 add_select_fusion.4
  193.0 1.0 add_select_fusion.4
  196.2 1.0 add_select_fusion.4
  206.8 1.0 add_select_fusion.4
  210.0 1.0 add_select_fusion.4
  217.4 1.0 add_select_fusion.4
  229.1 1.0 add_select_fusion.4
  237.6 1.0 add_select_fusion.4
  239.2 12.4 %psum.14 = f32[128]{0:T(128)S(1)} all-reduce(f32[128]{0:T(128)S(1)} %get-tuple-element.497), channel_id=1, replica_groups=mesh['ctx'=64,'tp'=8] {'tp'}, use_global_device_ids=true, to_apply=%region_3.4 | all-reduce | flops 128 | bytes 1024 | tf_op jit(solution)/shard_map/psum | solution.py:51
  251.8 12.6 %psum.15 = f32[128]{0:T(128)S(1)} all-reduce(f32[128]{0:T(128)S(1)} %fusion.30), channel_id=1, replica_groups=mesh['ctx'=64,'tp'=8] {'tp'}, use_global_device_ids=true, to_apply=%region_5.6 | all-reduce | flops 128 | bytes 1024 | tf_op jit(solution)/shard_map/psum | solution.py:56
  266.3 43.9 %all-gather.7.cloned.1.call-done = bf16[8192,128]{1,0:T(8,128)(2,1)} async-done(((bf16[128,128]{1,0:T(8,128)(2,1)}), bf16[8192,128]{1,0:T(8,128)(2,1)}) %all-gather.7.cloned.1.call-update) | async-done | bytes 2097168 | tf_op jit(solution)/shard_map/all_gather | solution.py:117
  310.2 139.9 %all-gather.9.cloned.1.call-done = bf16[8192,128]{1,0:T(8,128)(2,1)} async-done(((bf16[128,128]{1,0:T(8,128)(2,1)}), bf16[8192,128]{1,0:T(8,128)(2,1)}) %all-gather.9.cloned.1.call-update) | async-done | bytes 2097168 | tf_op jit(solution)/shard_map/all_gather | solution.py:118
  450.1 48.5 %while.50 = (s32[]{:T(128)}, f32[1,4,128]{2,1,0:T(4,128)S(1)}, f32[1,4,128]{2,1,0:T(4,128)S(1)}, f32[1,4,128,128]{3,2,1,0:T(8,128)S(1)}, s32[128]{0:T(128)S(1)},...) while((s32[]{:T(128)}, f32[1,4,128]{2,1,0:T(4,128)S(1)}, ...), condition=%wide.region_11.12_spmd.clone, body=%wide.region_8.11_spmd.clone.sunk | while | flops 136973952 | bytes 4363975 | solution.py:127
  450.3 1.2 fusion.88
  451.5 1.4 fusion.91
  453.3 1.2 fusion.88
  454.6 1.4 fusion.91
  456.3 1.2 fusion.88
  457.6 1.4 fusion.91
  459.4 1.2 fusion.88
  460.6 1.4 fusion.91
  462.4 1.2 fusion.88
  463.7 1.4 fusion.91
  465.4 1.2 fusion.88
  466.7 1.4 fusion.91
  468.5 1.2 fusion.88
  469.7 1.4 fusion.91
  471.5 1.2 fusion.88
  472.8 1.4 fusion.91
  474.5 1.2 fusion.88
  475.8 1.4 fusion.91
  477.6 1.2 fusion.88
  478.8 1.4 fusion.91
  480.6 1.2 fusion.88
  481.8 1.4 fusion.91
  483.6 1.2 fusion.88
  484.9 1.4 fusion.91
  486.7 1.2 fusion.88
  487.9 1.4 fusion.91
  489.7 1.2 fusion.88
  490.9 1.4 fusion.91
  492.7 1.2 fusion.88
  494.0 1.4 fusion.91
  495.8 1.2 fusion.88
  497.0 1.4 fusion.91
  501.5 104.3 %all-gather.13.cloned.1.call-done = bf16[256,128,128]{2,1,0:T(8,128)(2,1)} async-done(((bf16[4,128,128]{2,1,0:T(8,128)(2,1)}), bf16[256,128,128]{2,1,0:T(8,128)(2,1)}) %all-gather.13.cloned.1.call-update) | async-done | bytes 8388624 | tf_op jit(solution)/shard_map/all_gather | solution.py:21
  605.8 68.2 %while.49 = (s32[]{:T(128)}, f32[4,128,128]{2,1,0:T(8,128)S(1)}, s32[]{:T(128)}, bf16[64,4,128,128]{3,2,1,0:T(8,128)(2,1)}, s32[]{:T(128)}, /*index=5*/s32[]{:T(128)}, s32[]{:T(128)}, s32[]{:T(128)}) while((s32[]{:T(128)}, f32[4,128,128]{2,1,0:T(8,128)S(1)}, s32[]{:T(128)}, bf16[64,4,128,128]{3,2,1,0:T(8,128)(2,1)}, s32[]{:T(128)}, ...), condition=%wide.region_7.8_spmd.clone, body=%wide.region_6.7_spmd.clone.sunk | while | flops 262152 | bytes 655515 | solution.py:30
  (269 shorter events, 129.7 us)
Async XLA Ops:
  7.2 4.5 copy-start
  7.2 163.5 %all-gather.11.cloned.1.call-start = ((), (), s32[]{:S(2)}) async-start(), calls=%async_computation.2 | async-start | bytes 8519680 | tf_op jit(solution)/shard_map/all_gather | solution.py:21
  10.0 300.1 %all-gather.7.cloned.1.call-start = ((), (), s32[]{:S(2)}) async-start(), calls=%async_computation | async-start | bytes 2129920 | tf_op jit(solution)/shard_map/all_gather | solution.py:117
  10.8 439.3 %all-gather.9.cloned.1.call-start = ((), (), s32[]{:S(2)}) async-start(), calls=%async_computation.1 | async-start | bytes 2129920 | tf_op jit(solution)/shard_map/all_gather | solution.py:118
  11.5 594.3 %all-gather.13.cloned.1.call-start = ((), (), s32[]{:S(2)}) async-start(), calls=%async_computation.3 | async-start | bytes 8519680 | tf_op jit(solution)/shard_map/all_gather | solution.py:21
  170.7 80.9 %copy-start.2 = (bf16[128,512]{1,0:T(8,128)(2,1)S(1)}, bf16[128,512]{1,0:T(8,128)(2,1)}, u32[]{:S(2)}) copy-start(bf16[128,512]{1,0:T(8,128)(2,1)} %param.17) | copy-start | bytes 393220
  238.6 211.5 %copy-start.4 = (s32[128]{0:T(128)S(1)}, s32[128]{0:T(128)}, u32[]{:S(2)}) copy-start(s32[128]{0:T(128)} %param.21) | copy-start | bytes 1540
  450.1 49.4 %copy-start.1 = (bf16[128,512]{1,0:T(8,128)(2,1)S(1)}, bf16[128,512]{1,0:T(8,128)(2,1)}, u32[]{:S(2)}) copy-start(bf16[128,512]{1,0:T(8,128)(2,1)} %param.16) | copy-start | bytes 393220
  501.2 172.9 %copy-start.3 = (bf16[128,512]{1,0:T(8,128)(2,1)S(1)}, bf16[128,512]{1,0:T(8,128)(2,1)}, u32[]{:S(2)}) copy-start(bf16[128,512]{1,0:T(8,128)(2,1)} %param.15) | copy-start | bytes 393220
Sparse Core Ops, SparseCore 0:
  11.5 159.1 all-gather.10
  173.7 136.4 all-gather.6
  313.1 136.9 all-gather.8
  453.5 152.2 all-gather.12
where the time goes:
time: 688 us; the launch traced here: 683 us
  waiting for transfers between devices  445 us (65%)
  other arithmetic  140 us (20%)
  matrix products  47.7 us (7%)
  blocking collectives  25.1 us (4%)
  between operations  14 us (2%)
    all_gather x2, waiting for transfers between devices, carried_in(): everything = lax.all_gather(value.astype(jnp.bfloat16), axis)  260 us
    all_gather x1, waiting for transfers between devices, on_device(): value_rows = lax.all_gather(soft_value, 'ctx', axis=0, tiled=True)  140 us
    select_n x128, other arithmetic, hop(): return jnp.where(reached, new, before)  133 us
    all_gather x1, waiting for transfers between devices, on_device(): key_rows = lax.all_gather(soft_key, 'ctx', axis=0, tiled=True)  43.9 us
    dot_general x16, matrix products, attend(): jnp.einsum('kgtn,nkd->kgtd', probs.astype(jnp.bfloat16), value_heads, pre...  21.7 us
    dot_general x16, matrix products, attend(): jnp.einsum('tkgd,nkd->kgtn', soft_q, key_heads, preferred_element_type=jn...  19.6 us
  transfers between devices with their start and end apart: 4, of which 4 were waited for; matrix products, arithmetic and copies ran while one was open for 18% of the time, Pallas kernels for 0%

commit v1 on v0

v1 whole, which is shorter than its diff:
```python
import functools
import math

import jax
import jax.numpy as jnp
from jax import lax
from jax.experimental import pallas as pl
from jax.experimental.pallas import tpu as pltpu
from jax.sharding import PartitionSpec as P

HD = 128
LH = 32
SH = 32
KVH = 8
T = 128
HERE = 4
TP = 8
NY = 4
NZ = 16
PIECE = HERE * HD // NZ
CHUNK = 4

epsilon = 1e-06
floor_score = -1e30
bf16 = jnp.bfloat16
f32 = jnp.float32

z_groups = [[y * NZ + z for z in range(NZ)] for y in range(NY)]


def y_shift(step):
    return [(i, i + NZ * step) for i in range(NY * NZ) if 0 <= i + NZ * step < NY * NZ]


def dot(a, b, contract_a, contract_b):
    return lax.dot_general(
        a, b, (((contract_a,), (contract_b,)), ((), ())), preferred_element_type=f32
    )


def call(kernel, outs, *args, flops=1e8, name=None, vmem=48 * 2**20, scratch=(), smem=()):
    size = sum(a.size * a.dtype.itemsize for a in args)
    size += sum(math.prod(s) * jnp.dtype(d).itemsize for s, d in outs)
    specs = [
        pl.BlockSpec(memory_space=pltpu.SMEM if i in smem else pltpu.VMEM)
        for i in range(len(args))
    ]
    out = pl.pallas_call(
        kernel,
        out_shape=[jax.ShapeDtypeStruct(s, d) for s, d in outs],
        in_specs=specs,
        out_specs=[pl.BlockSpec(memory_space=pltpu.VMEM) for _ in outs],
        scratch_shapes=list(scratch),
        compiler_params=pltpu.CompilerParams(vmem_limit_bytes=vmem),
        cost_estimate=pl.CostEstimate(flops=int(flops), bytes_accessed=size, transcendentals=0),
        name=name,
    )(*args)
    return out


def head(ref, h):
    return ref[:, h * HD : (h + 1) * HD]


def state_of(ref, h):
    per = HD // PIECE
    return ref[h * per : (h + 1) * per].reshape(HD, HD)


def put_state(ref, h, value):
    per = HD // PIECE
    ref[h * per : (h + 1) * per] = value.astype(bf16).reshape(per, PIECE, HD)


def lower_triangle():
    rows = lax.broadcasted_iota(jnp.int32, (T, T), 0)
    cols = lax.broadcasted_iota(jnp.int32, (T, T), 1)
    return cols <= rows


def own_kernel(k, v, sk, sv, own, kv):
    kv[0] = sk[...]
    kv[1] = sv[...]
    for h in range(HERE):
        put_state(own, h, dot(head(k, h), head(v, h), 0, 0))


def local_kernel(q, k, v, weights, local):
    lower = lower_triangle()
    for h in range(HERE):
        w = jnp.where(lower, dot(head(q, h), head(k, h), 1, 1), 0.0).astype(bf16)
        weights[h] = w
        local[:, h * HD : (h + 1) * HD] = dot(w, head(v, h), 1, 0)


def total_kernel(r, tot):
    acc = r[0].astype(f32)
    for i in range(1, NZ):
        acc = acc + r[i].astype(f32)
    tot[...] = acc.astype(bf16)


def carry_kernel(reverse, r, a, b, c, out):
    acc = a[...].astype(f32) + b[...].astype(f32) + c[...].astype(f32)
    for i in reversed(range(NZ)) if reverse else range(NZ):
        out[i] = acc.astype(bf16)
        acc = acc + r[i].astype(f32)


def mix_kernel(q, g, local, s, mix, sums):
    squares = jnp.zeros((T, HD), f32)
    inner = jnp.zeros((T, HD), f32)
    for h in range(HERE):
        m = head(local, h) + dot(head(q, h), state_of(s, h), 1, 0)
        mix[:, h * HD : (h + 1) * HD] = m
        squares = squares + m * m
        inner = inner + m * head(g, h).astype(f32)
    lane = lax.broadcasted_iota(jnp.int32, (T, HD), 1)
    both = jnp.where(
        lane == 0,
        jnp.sum(squares, axis=1, keepdims=True),
        jnp.where(lane == 1, jnp.sum(inner, axis=1, keepdims=True), 0.0),
    )
    rows = jnp.transpose(both)[0:8]
    for i in range(TP):
        sums[i] = rows


def norm_kernel(q, g, mix, sums, lin_out, grad_mix, own):
    rows = sums[0]
    for i in range(1, TP):
        rows = rows + sums[i]
    cols = jnp.transpose(jnp.concatenate([rows, jnp.zeros((T - 8, HD), f32)], axis=0))
    scale = lax.rsqrt(cols[:, 0:1] / (LH * HD) + epsilon)
    c = scale * cols[:, 1:2] / (LH * HD)
    for h in range(HERE):
        normed = head(mix, h) * scale
        lin_out[:, h * HD : (h + 1) * HD] = normed.astype(bf16)
        gm = (scale * (head(g, h).astype(f32) - normed * c)).astype(bf16)
        grad_mix[:, h * HD : (h + 1) * HD] = gm
        put_state(own, h, dot(head(q, h), gm, 0, 0))


def inside_kernel(q, k, v, gm, weights, s, grad_q, part_k, part_v):
    lower = lower_triangle()
    for h in range(HERE):
        at = slice(h * HD, (h + 1) * HD)
        gs = jnp.where(lower, dot(head(gm, h), head(v, h), 1, 1), 0.0).astype(bf16)
        gq = dot(gs, head(k, h), 1, 0) + dot(head(gm, h), state_of(s, h), 1, 1)
        grad_q[:, at] = gq.astype(bf16)
        part_k[:, at] = dot(gs, head(q, h), 0, 0)
        part_v[:, at] = dot(weights[h], head(gm, h), 0, 0)


def final_kernel(k, v, part_k, part_v, a, grad_k, grad_v):
    for h in range(HERE):
        at = slice(h * HD, (h + 1) * HD)
        later = state_of(a, h)
        grad_k[:, at] = (head(part_k, h) + dot(head(v, h), later, 1, 1)).astype(bf16)
        grad_v[:, at] = (head(part_v, h) + dot(head(k, h), later, 1, 0)).astype(bf16)


def soft_kernel(q, kv, doc_row, doc, out, qs, top, total, acc):
    me = lax.axis_index("ctx")
    my_y = me // NZ
    keys = CHUNK * T
    width = HERE * T
    factor = math.log2(math.e) / math.sqrt(HD)
    for h in range(HERE):
        qs[h * T : (h + 1) * T] = head(q, h)
    top[...] = jnp.full((1, width), floor_score, f32)
    total[...] = jnp.zeros((1, width), f32)
    acc[...] = jnp.zeros((HD, width), f32)
    first_chunk = doc[0] // keys
    my_chunk = me // CHUNK
    last_start = doc[T - 1]

    def visit(chunk, masked):
        block = chunk * CHUNK
        slot = my_y - block // NZ
        z0 = lax.rem(block, NZ)
        k = kv[pl.ds(z0, CHUNK), slot, 0].reshape(keys, HD)
        v = kv[pl.ds(z0, CHUNK), slot, 1].reshape(keys, HD)
        scores = dot(k, qs[...], 1, 1)
        if masked:
            key_pos = chunk * keys + lax.broadcasted_iota(jnp.int32, (keys, width), 0)
            query_pos = me * T + lax.rem(
                lax.broadcasted_iota(jnp.int32, (1, width), 1), jnp.int32(T)
            )
            starts = jnp.concatenate([doc_row[...]] * HERE, axis=1)
            allowed = (key_pos <= query_pos) & (key_pos >= starts)
            scores = jnp.where(allowed, scores, 2 * floor_score)
        old_top = top[...]
        new_top = jnp.maximum(old_top, jnp.max(scores, axis=0, keepdims=True))
        probs = jnp.exp2((scores - new_top) * factor)
        shrink = jnp.exp2((old_top - new_top) * factor)
        top[...] = new_top
        total[...] = shrink * total[...] + jnp.sum(probs, axis=0, keepdims=True)
        acc[...] = shrink * acc[...] + dot(v, probs.astype(bf16), 0, 0)

    def step(chunk, carry):
        clear = (chunk < my_chunk) & (chunk * keys >= last_start)

        @pl.when(clear)
        def _():
            visit(chunk, False)

        @pl.when(jnp.logical_not(clear))
        def _():
            visit(chunk, True)

        return carry

    lax.fori_loop(first_chunk, my_chunk + 1, step, 0)
    result = acc[...] / total[...]
    for h in range(HERE):
        out[:, h * HD : (h + 1) * HD] = jnp.transpose(result[:, h * T : (h + 1) * T]).astype(bf16)


def carried_in(own, reverse):
    pieces = (NZ, PIECE, HD)
    tag = "later" if reverse else "earlier"
    swap = functools.partial(
        lax.all_to_all,
        axis_name="ctx",
        split_axis=0,
        concat_axis=0,
        tiled=True,
        axis_index_groups=z_groups,
    )
    got = swap(own)
    (line,) = call(total_kernel, [((PIECE, HD), bf16)], got, flops=1e5, name=tag + "_total")
    sign = -1 if reverse else 1
    rows = [lax.ppermute(line, "ctx", y_shift(sign * s)) for s in (1, 2, 3)]
    (carried,) = call(
        functools.partial(carry_kernel, reverse),
        [(pieces, bf16)],
        got,
        *rows,
        flops=1e5,
        name=tag + "_carry",
    )
    return swap(carried)


def on_device(
    lin_query, lin_key, lin_value, lin_cotangent, soft_query, soft_key, soft_value, doc_start
):
    q, k, v, g = lin_query, lin_key, lin_value, lin_cotangent
    wide = (T, HERE * HD)
    states = (NZ, PIECE, HD)
    squares = (HERE, T, T)
    own, kv = call(
        own_kernel,
        [(states, bf16), ((2, T, HD), bf16)],
        k,
        v,
        soft_key,
        soft_value,
        name="own_state",
    )
    slots = [kv] + [lax.ppermute(kv, "ctx", y_shift(s)) for s in (1, 2, 3)]
    all_kv = lax.all_gather(jnp.stack(slots), "ctx", axis_index_groups=z_groups)
    weights, local = call(
        local_kernel, [(squares, bf16), (wide, f32)], q, k, v, name="local"
    )
    earlier = carried_in(own, False)
    mix, sums = call(
        mix_kernel, [(wide, f32), ((TP, 8, HD), f32)], q, g, local, earlier, name="mix"
    )
    sums = lax.all_to_all(sums, "tp", 0, 0, tiled=True)
    lin_out, gm, own_adjoint = call(
        norm_kernel,
        [(wide, bf16), (wide, bf16), (states, bf16)],
        q,
        g,
        mix,
        sums,
        name="norm",
    )
    later = carried_in(own_adjoint, True)
    grad_query, part_k, part_v = call(
        inside_kernel,
        [(wide, bf16), (wide, f32), (wide, f32)],
        q,
        k,
        v,
        gm,
        weights,
        earlier,
        name="inside",
    )
    grad_key, grad_value = call(
        final_kernel, [(wide, bf16), (wide, bf16)], k, v, part_k, part_v, later, name="final"
    )
    (soft_out,) = call(
        soft_kernel,
        [(wide, bf16)],
        soft_query,
        all_kv,
        doc_start.reshape(1, T),
        doc_start,
        smem=(3,),
        flops=1e9,
        scratch=[
            pltpu.VMEM((HERE * T, HD), bf16),
            pltpu.VMEM((1, HERE * T), f32),
            pltpu.VMEM((1, HERE * T), f32),
            pltpu.VMEM((HD, HERE * T), f32),
        ],
        name="soft",
    )
    return (lin_out, grad_query, grad_key, grad_value, soft_out)


def solution(mesh):
    wide = P("ctx", "tp")
    return jax.shard_map(
        on_device,
        mesh=mesh,
        in_specs=(wide,) * 7 + (P("ctx"),),
        out_specs=(wide,) * 5,
        check_vma=False,
    )
```

time: 688 us -> 157 us (0.23)
  waiting for transfers between devices: 445 us -> 35.8 us
  other arithmetic: 140 us -> 0.75 us
  matrix products: 47.7 us -> 0 us
  blocking collectives: 25.1 us -> 55.7 us
  starting transfers between devices: 0.16 us -> 24.5 us
  Pallas kernels: 0 us -> 14.2 us
    all_gather x4 -> x1, waiting for transfers between devices: 444 us -> 0.01 us  [on_device(): all_kv = lax.all_gather(jnp.stack(slots), 'ctx', axis_index_groups=z_groups)]
    select_n x128 -> x0, other arithmetic: 133 us -> none  [hop(): return jnp.where(reached, new, before)]
    all_to_all x0 -> x3, blocking collectives: none -> 55.7 us  [the longest x2 46.2 us: carried_in(): got = swap(own)]
    dot_general x44 -> x0, matrix products: 47.7 us -> none  [the longest x16 21.7 us: attend(): jnp.einsum('kgtn,nkd->kgtd', probs.astype(jnp.bfloat16), value_heads, pre...]
    psum x2 -> x0, blocking collectives: 25.1 us -> none  [the longest x1 12.6 us: on_device(): inner = lax.psum(jnp.sum(grad * normed, axis=1), 'tp')]
    all_to_all x0 -> x2, waiting for transfers between devices: none -> 24.2 us  [carried_in(): return swap(carried)]
    ppermute x0 -> x9, starting transfers between devices: none -> 16.4 us  [the longest x6 12.5 us: carried_in(): rows = [lax.ppermute(line, 'ctx', y_shift(sign * s)) for s in (1, 2, 3)]]
    pallas_call x0 -> x11, Pallas kernels: none -> 14.2 us  [call(): pl.pallas_call(kernel, out_shape=[jax.ShapeDtypeStruct(s, d) for s, d in...]
  transfers between devices with their start and end apart: 4 -> 12, of which waited for: 4 -> 6; matrix products, arithmetic and copies ran while one was open for 18% -> 0% of each run, Pallas kernels for 0% -> 4%
where the time goes in v1:
time: 157 us; the launch traced here: 156 us
  blocking collectives  55.7 us (35%)
  waiting for transfers between devices  35.8 us (23%)
  starting transfers between devices  24.5 us (16%)
  Pallas kernels  14.2 us (9%)
  between operations  14.2 us (9%)
  local copies, waits for them, and re-layouts  11 us (7%)
    all_to_all x2, blocking collectives, carried_in(): got = swap(own)  46.2 us
    all_to_all x2, waiting for transfers between devices, carried_in(): return swap(carried)  24.2 us
    pallas_call x11, Pallas kernels, call(): pl.pallas_call(kernel, out_shape=[jax.ShapeDtypeStruct(s, d) for s, d in...  14.2 us
    ppermute x6, starting transfers between devices, carried_in(): rows = [lax.ppermute(line, 'ctx', y_shift(sign * s)) for s in (1, 2, 3)]  12.5 us
    unnamed x32, local copies, waits for them, and re-layouts  11 us
    all_to_all x1, blocking collectives, on_device(): sums = lax.all_to_all(sums, 'tp', 0, 0, tiled=True)  9.52 us
    all_to_all x2, starting transfers between devices, carried_in(): return swap(carried)  8.13 us
    ppermute x6, waiting for transfers between devices, carried_in(): rows = [lax.ppermute(line, 'ctx', y_shift(sign * s)) for s in (1, 2, 3)]  5.78 us
  transfers between devices with their start and end apart: 12, of which 6 were waited for; matrix products, arithmetic and copies ran while one was open for 0% of the time, Pallas kernels for 4%

profile of v1, /device:TPU:24, one launch (start us, length us, event | category | flops | bytes accessed | tf_op | source)
XLA Modules:
  0.0 156.2 jit_solution(17409790218900668927)
XLA Ops:
  7.2 0.0 copy-start.3
  7.2 0.0 all-gather.3.cloned.1.call-start
  7.2 0.0 copy-start.4
  7.2 0.9 copy-done.4
  8.2 0.0 copy-start.7
  8.2 0.9 copy-done.7
  9.1 0.0 copy-start.14
  9.1 0.8 copy-done.14
  9.8 0.0 copy-start.15
  9.8 0.8 copy-done.15
  10.6 0.0 copy-start.6
  10.6 0.0 copy-start.9
  10.6 0.0 copy-start.12
  10.6 0.2 own_state.1
  10.8 1.3 collective-permute-start.8
  12.1 1.3 collective-permute-start.7
  13.4 1.3 collective-permute-start.6
  14.7 5.8 %collective-permute-done.8 = bf16[2,128,128]{2,1,0:T(8,128)(2,1)S(1)} collective-permute-done((bf16[2,128,128]{2,1,0:T(8,128)(2,1)S(1)}, bf16[2,128,128]{2,1,0:T(8,128)(2,1)S(1)}, u32[]{:S(2)}, u32[]{:S(2)}) %collective-permute-start.8) | collective-permute-done | bytes 65568 | tf_op jit(solution)/shard_map/ppermute | solution.py:262
  20.5 0.0 collective-permute-done.7
  20.5 0.0 collective-permute-done.6
  20.5 0.8 pad_maximum_fusion
  21.2 0.0 all-gather.3.cloned.1.call-update
  21.3 28.3 %all_to_all.25.r = bf16[16,32,128]{2,1,0:T(8,128)(2,1)S(1)} all-to-all(bf16[16,32,128]{2,1,0:T(8,128)(2,1)S(1)} %get-tuple-element.20), channel_id=1, replica_groups={{0,8,16,24,32,40,48,56,64,72,80,88,96,104,112,120},{128,136,144,152,160..., dimensions={0} | all-to-all | bytes 262144 | tf_op jit(solution)/shard_map/all_to_all | solution.py:231
  49.6 1.3 collective-permute-start.2
  50.9 1.3 collective-permute-start.1
  52.2 1.3 collective-permute-start
  53.5 2.9 %collective-permute-done.2.c = bf16[32,128]{1,0:T(8,128)(2,1)S(1)} collective-permute-done((bf16[32,128]{1,0:T(8,128)(2,1)S(1)}, bf16[32,128]{1,0:T(8,128)(2,1)S(1)}, u32[]{:S(2)}, u32[]{:S(2)}) %collective-permute-start.2) | collective-permute-done | bytes 8224 | tf_op jit(solution)/shard_map/ppermute | solution.py:234
  56.3 1.6 %collective-permute-done.1.b = bf16[32,128]{1,0:T(8,128)(2,1)S(1)} collective-permute-done((bf16[32,128]{1,0:T(8,128)(2,1)S(1)}, bf16[32,128]{1,0:T(8,128)(2,1)S(1)}, u32[]{:S(2)}, u32[]{:S(2)}) %collective-permute-start.1) | collective-permute-done | bytes 8224 | tf_op jit(solution)/shard_map/ppermute | solution.py:234
  57.9 0.0 collective-permute-done.a
  57.9 0.7 earlier_carry.1
  58.6 3.6 %all-to-all-start.1 = ((bf16[16,32,128]{2,1,0:T(8,128)(2,1)}), bf16[16,32,128]{2,1,0:T(8,128)(2,1)S(1)}, u32[]{:S(2)}, u32[]{:S(2)}) async-start(bf16[16,32,128]{2,1,0:T(8,128)(2,1)} %earlier_carry.1), calls=%async_computation.1 | async-start | bytes 262144 | tf_op jit(solution)/shard_map/all_to_all | solution.py:243
  62.2 0.0 copy-start.1
  62.2 0.9 copy-done.1
  63.1 0.0 copy-start.5
  63.1 0.9 copy-done.5
  64.0 0.9 copy-done.8
  64.9 0.7 local.1
  65.7 11.7 %all-to-all-done.1.s = bf16[16,32,128]{2,1,0:T(8,128)(2,1)S(1)} async-done(((bf16[16,32,128]{2,1,0:T(8,128)(2,1)}), bf16[16,32,128]{2,1,0:T(8,128)(2,1)S(1)}, u32[]{:S(2)}, u32[]{:S(2)}) %all-to-all-start.1) | async-done | bytes 131104 | tf_op jit(solution)/shard_map/all_to_all | solution.py:243
  77.4 0.9 copy-done.2
  78.3 0.9 copy-done.10
  79.2 0.3 mix.1
  79.5 9.5 %all_to_all.26.sums = f32[8,8,128]{2,1,0:T(8,128)S(1)} all-to-all(f32[8,8,128]{2,1,0:T(8,128)S(1)} %get-tuple-element.22), channel_id=1, replica_groups=mesh['ctx'=64,'tp'=8] {'tp'}, dimensions={0} | all-to-all | bytes 65536 | tf_op jit(solution)/shard_map/all_to_all | solution.py:271
  89.1 0.9 copy-done.11
  90.0 0.9 norm.1
  90.9 18.0 %all_to_all.27.r = bf16[16,32,128]{2,1,0:T(8,128)(2,1)S(1)} all-to-all(bf16[16,32,128]{2,1,0:T(8,128)(2,1)S(1)} %get-tuple-element.29), channel_id=1, replica_groups={{0,8,16,24,32,40,48,56,64,72,80,88,96,104,112,120},{128,136,144,152,160..., dimensions={0} | all-to-all | bytes 262144 | tf_op jit(solution)/shard_map/all_to_all | solution.py:231
  108.9 4.6 %collective-permute-start.5 = (bf16[32,128]{1,0:T(8,128)(2,1)S(1)}, bf16[32,128]{1,0:T(8,128)(2,1)S(1)}, u32[]{:S(2)}, u32[]{:S(2)}) collective-permute-start(bf16[32,128]{1,0:T(8,128)(2,1)S(1)} %later_total.1), channel_id=1, source_target_pairs={{384,0},{392,8},{400,16},{408,24},{416,32},{424,40},{432,48},{440,... | collective-permute-start | bytes 24584 | tf_op jit(solution)/shard_map/ppermute | solution.py:234
  113.4 2.6 %collective-permute-start.4 = (bf16[32,128]{1,0:T(8,128)(2,1)S(1)}, bf16[32,128]{1,0:T(8,128)(2,1)S(1)}, u32[]{:S(2)}, u32[]{:S(2)}) collective-permute-start(bf16[32,128]{1,0:T(8,128)(2,1)S(1)} %later_total.1), channel_id=1, source_target_pairs={{256,0},{264,8},{272,16},{280,24},{288,32},{296,40},{304,48},{312,... | collective-permute-start | bytes 24584 | tf_op jit(solution)/shard_map/ppermute | solution.py:234
  116.0 1.5 collective-permute-start.3
  117.5 0.0 collective-permute-done.5.c
  117.5 0.0 collective-permute-done.4.b
  117.5 1.3 collective-permute-done.3.a
  118.9 0.7 later_carry.1
  119.5 4.5 %all-to-all-start.4 = ((bf16[16,32,128]{2,1,0:T(8,128)(2,1)}), bf16[16,32,128]{2,1,0:T(8,128)(2,1)S(1)}, u32[]{:S(2)}, u32[]{:S(2)}) async-start(bf16[16,32,128]{2,1,0:T(8,128)(2,1)} %later_carry.1), calls=%async_computation.4 | async-start | bytes 262144 | tf_op jit(solution)/shard_map/all_to_all | solution.py:243
  124.1 0.0 copy-done.3
  124.1 0.0 copy-done.6
  124.1 0.0 copy-done.9
  124.1 1.4 inside.1
  125.5 12.5 %all-to-all-done.4.a = bf16[16,32,128]{2,1,0:T(8,128)(2,1)S(1)} async-done(((bf16[16,32,128]{2,1,0:T(8,128)(2,1)}), bf16[16,32,128]{2,1,0:T(8,128)(2,1)S(1)}, u32[]{:S(2)}, u32[]{:S(2)}) %all-to-all-start.4) | async-done | bytes 131104 | tf_op jit(solution)/shard_map/all_to_all | solution.py:243
  137.9 0.9 final.1
  138.9 0.0 copy-done.12
  138.9 0.0 copy-done.13
  138.9 0.0 copy-start
  138.9 2.2 %copy-done = bf16[64,2,128,128]{3,2,1,0:T(8,128)(2,1)S(1)} copy-done((bf16[64,2,128,128]{3,2,1,0:T(8,128)(2,1)S(1)}, bf16[64,2,128,128]{3,2,1,0:T(8,128)(2,1)}, u32[]{:S(2)}) %copy-start) | copy-done | bytes 4194328
  141.1 8.2 %soft.1 = bf16[128,512]{1,0:T(8,128)(2,1)} custom-call(bf16[128,512]{1,0:T(8,128)(2,1)S(1)} %copy-done.12, bf16[16,4,2,128,128]{4,3,2,1,0:T(8,128)(2,1)S(1)} %bitcast.6, s32[1,128]{1,0:T(1,128)S(1)} %bitcast.8, s32[128]{0:T(128)S(1)} %copy-done.13), custom_call_target="tpu_custom_call" | custom-call | flops 1000000000 | bytes 4457472 | tf_op jit(solution)/shard_map/soft/pallas_call | solution.py:48
  (8 shorter events, 0.1 us)
Async XLA Ops:
  7.2 116.9 %copy-start.3 = (bf16[128,512]{1,0:T(8,128)(2,1)S(1)}, bf16[128,512]{1,0:T(8,128)(2,1)}, u32[]{:S(2)}) copy-start(bf16[128,512]{1,0:T(8,128)(2,1)} %q.8) | copy-start | bytes 393220
  7.2 131.7 %all-gather.3.cloned.1.call-start = ((), (), s32[]{:S(2)}) async-start(), calls=%async_computation.5 | async-start | bytes 4456448 | tf_op jit(solution)/shard_map/all_gather | solution.py:263
  7.2 0.9 copy-start.4
  8.2 0.9 copy-start.7
  9.1 0.8 copy-start.14
  9.8 0.8 copy-start.15
  10.6 113.5 %copy-start.6 = (bf16[128,512]{1,0:T(8,128)(2,1)S(1)}, bf16[128,512]{1,0:T(8,128)(2,1)}, u32[]{:S(2)}) copy-start(bf16[128,512]{1,0:T(8,128)(2,1)} %k.7) | copy-start | bytes 393220
  10.6 113.5 %copy-start.9 = (bf16[128,512]{1,0:T(8,128)(2,1)S(1)}, bf16[128,512]{1,0:T(8,128)(2,1)}, u32[]{:S(2)}) copy-start(bf16[128,512]{1,0:T(8,128)(2,1)} %v.7) | copy-start | bytes 393220
  10.6 128.3 %copy-start.12 = (bf16[128,512]{1,0:T(8,128)(2,1)S(1)}, bf16[128,512]{1,0:T(8,128)(2,1)}, u32[]{:S(2)}) copy-start(bf16[128,512]{1,0:T(8,128)(2,1)} %q.9) | copy-start | bytes 393220
  10.6 128.3 %copy-start.13 = (s32[128]{0:T(128)S(1)}, s32[128]{0:T(128)}, u32[]{:S(2)}) copy-start(s32[128]{0:T(128)} %doc.1) | copy-start | bytes 1540
  10.8 9.7 %collective-permute-start.8 = (bf16[2,128,128]{2,1,0:T(8,128)(2,1)S(1)}, bf16[2,128,128]{2,1,0:T(8,128)(2,1)S(1)}, u32[]{:S(2)}, u32[]{:S(2)}) collective-permute-start(bf16[2,128,128]{2,1,0:T(8,128)(2,1)S(1)} %get-tuple-element.32), channel_id=1, source_target_pairs={{0,384},{8,392},{16,400},{24,408},{32,416},{40,424},{48,432},{56,4... | collective-permute-start | bytes 196616 | tf_op jit(solution)/shard_map/ppermute | solution.py:262
  12.1 8.4 %collective-permute-start.7 = (bf16[2,128,128]{2,1,0:T(8,128)(2,1)S(1)}, bf16[2,128,128]{2,1,0:T(8,128)(2,1)S(1)}, u32[]{:S(2)}, u32[]{:S(2)}) collective-permute-start(bf16[2,128,128]{2,1,0:T(8,128)(2,1)S(1)} %get-tuple-element.32), channel_id=1, source_target_pairs={{0,256},{8,264},{16,272},{24,280},{32,288},{40,296},{48,304},{56,3... | collective-permute-start | bytes 196616 | tf_op jit(solution)/shard_map/ppermute | solution.py:262
  13.4 7.1 %collective-permute-start.6 = (bf16[2,128,128]{2,1,0:T(8,128)(2,1)S(1)}, bf16[2,128,128]{2,1,0:T(8,128)(2,1)S(1)}, u32[]{:S(2)}, u32[]{:S(2)}) collective-permute-start(bf16[2,128,128]{2,1,0:T(8,128)(2,1)S(1)} %get-tuple-element.32), channel_id=1, source_target_pairs={{0,128},{8,136},{16,144},{24,152},{32,160},{40,168},{48,176},{56,1... | collective-permute-start | bytes 196616 | tf_op jit(solution)/shard_map/ppermute | solution.py:262
  49.6 6.8 %collective-permute-start.2 = (bf16[32,128]{1,0:T(8,128)(2,1)S(1)}, bf16[32,128]{1,0:T(8,128)(2,1)S(1)}, u32[]{:S(2)}, u32[]{:S(2)}) collective-permute-start(bf16[32,128]{1,0:T(8,128)(2,1)S(1)} %earlier_total.1), channel_id=1, source_target_pairs={{0,384},{8,392},{16,400},{24,408},{32,416},{40,424},{48,432},{56,4... | collective-permute-start | bytes 24584 | tf_op jit(solution)/shard_map/ppermute | solution.py:234
  50.9 7.0 %collective-permute-start.1 = (bf16[32,128]{1,0:T(8,128)(2,1)S(1)}, bf16[32,128]{1,0:T(8,128)(2,1)S(1)}, u32[]{:S(2)}, u32[]{:S(2)}) collective-permute-start(bf16[32,128]{1,0:T(8,128)(2,1)S(1)} %earlier_total.1), channel_id=1, source_target_pairs={{0,256},{8,264},{16,272},{24,280},{32,288},{40,296},{48,304},{56,3... | collective-permute-start | bytes 24584 | tf_op jit(solution)/shard_map/ppermute | solution.py:234
  52.2 5.8 %collective-permute-start = (bf16[32,128]{1,0:T(8,128)(2,1)S(1)}, bf16[32,128]{1,0:T(8,128)(2,1)S(1)}, u32[]{:S(2)}, u32[]{:S(2)}) collective-permute-start(bf16[32,128]{1,0:T(8,128)(2,1)S(1)} %earlier_total.1), channel_id=1, source_target_pairs={{0,128},{8,136},{16,144},{24,152},{32,160},{40,168},{48,176},{56,1... | collective-permute-start | bytes 24584 | tf_op jit(solution)/shard_map/ppermute | solution.py:234
  58.6 18.8 %all-to-all-start.1 = ((bf16[16,32,128]{2,1,0:T(8,128)(2,1)}), bf16[16,32,128]{2,1,0:T(8,128)(2,1)S(1)}, u32[]{:S(2)}, u32[]{:S(2)}) async-start(bf16[16,32,128]{2,1,0:T(8,128)(2,1)} %earlier_carry.1), calls=%async_computation.1 | async-start | bytes 262144 | tf_op jit(solution)/shard_map/all_to_all | solution.py:243
  62.2 0.9 copy-start.1
  63.1 0.9 copy-start.5
  64.0 0.9 copy-start.8
  77.4 0.9 copy-start.2
  78.3 0.9 copy-start.10
  89.1 0.9 copy-start.11
  108.9 8.6 %collective-permute-start.5 = (bf16[32,128]{1,0:T(8,128)(2,1)S(1)}, bf16[32,128]{1,0:T(8,128)(2,1)S(1)}, u32[]{:S(2)}, u32[]{:S(2)}) collective-permute-start(bf16[32,128]{1,0:T(8,128)(2,1)S(1)} %later_total.1), channel_id=1, source_target_pairs={{384,0},{392,8},{400,16},{408,24},{416,32},{424,40},{432,48},{440,... | collective-permute-start | bytes 24584 | tf_op jit(solution)/shard_map/ppermute | solution.py:234
  113.4 4.1 %collective-permute-start.4 = (bf16[32,128]{1,0:T(8,128)(2,1)S(1)}, bf16[32,128]{1,0:T(8,128)(2,1)S(1)}, u32[]{:S(2)}, u32[]{:S(2)}) collective-permute-start(bf16[32,128]{1,0:T(8,128)(2,1)S(1)} %later_total.1), channel_id=1, source_target_pairs={{256,0},{264,8},{272,16},{280,24},{288,32},{296,40},{304,48},{312,... | collective-permute-start | bytes 24584 | tf_op jit(solution)/shard_map/ppermute | solution.py:234
  116.0 2.8 %collective-permute-start.3 = (bf16[32,128]{1,0:T(8,128)(2,1)S(1)}, bf16[32,128]{1,0:T(8,128)(2,1)S(1)}, u32[]{:S(2)}, u32[]{:S(2)}) collective-permute-start(bf16[32,128]{1,0:T(8,128)(2,1)S(1)} %later_total.1), channel_id=1, source_target_pairs={{128,0},{136,8},{144,16},{152,24},{160,32},{168,40},{176,48},{184,... | collective-permute-start | bytes 24584 | tf_op jit(solution)/shard_map/ppermute | solution.py:234
  119.5 18.4 %all-to-all-start.4 = ((bf16[16,32,128]{2,1,0:T(8,128)(2,1)}), bf16[16,32,128]{2,1,0:T(8,128)(2,1)S(1)}, u32[]{:S(2)}, u32[]{:S(2)}) async-start(bf16[16,32,128]{2,1,0:T(8,128)(2,1)} %later_carry.1), calls=%async_computation.4 | async-start | bytes 262144 | tf_op jit(solution)/shard_map/all_to_all | solution.py:243
  138.9 2.2 %copy-start = (bf16[64,2,128,128]{3,2,1,0:T(8,128)(2,1)S(1)}, bf16[64,2,128,128]{3,2,1,0:T(8,128)(2,1)}, u32[]{:S(2)}) copy-start(bf16[64,2,128,128]{3,2,1,0:T(8,128)(2,1)} %all-gather.3.cloned.1.call-done) | copy-start | bytes 12582916
Sparse Core Ops, SparseCore 0:
  21.4 92.2 all-gather.2

commit v2 on v1

--- a/solution.py
+++ b/solution.py
@@ -20,6 +20,9 @@
 PIECE = HERE * HD // NZ
 CHUNK = 4
 
+BIG = 60 * 2**20
+COST = dict(own=1e8, local=1e8, total=1e10, carry=1e10, mix=1.6e10, norm=1.6e10, inside=1e8, final=1e8, soft=1e8)
+
 epsilon = 1e-06
 floor_score = -1e30
 bf16 = jnp.bfloat16
@@ -38,18 +41,21 @@
     )
 
 
-def call(kernel, outs, *args, flops=1e8, name=None, vmem=48 * 2**20, scratch=(), smem=()):
+def call(kernel, outs, *args, flops=1e8, name=None, vmem=16 * 2**20, scratch=(), smem=(), far=(), far_out=()):
     size = sum(a.size * a.dtype.itemsize for a in args)
     size += sum(math.prod(s) * jnp.dtype(d).itemsize for s, d in outs)
     specs = [
-        pl.BlockSpec(memory_space=pltpu.SMEM if i in smem else pltpu.VMEM)
+        pl.BlockSpec(memory_space=pltpu.SMEM if i in smem else pltpu.HBM if i in far else pltpu.VMEM)
         for i in range(len(args))
     ]
     out = pl.pallas_call(
         kernel,
         out_shape=[jax.ShapeDtypeStruct(s, d) for s, d in outs],
         in_specs=specs,
-        out_specs=[pl.BlockSpec(memory_space=pltpu.VMEM) for _ in outs],
+        out_specs=[
+            pl.BlockSpec(memory_space=pltpu.HBM if i in far_out else pltpu.VMEM)
+            for i in range(len(outs))
+        ],
         scratch_shapes=list(scratch),
         compiler_params=pltpu.CompilerParams(vmem_limit_bytes=vmem),
         cost_estimate=pl.CostEstimate(flops=int(flops), bytes_accessed=size, transcendentals=0),
@@ -78,14 +84,26 @@
     return cols <= rows
 
 
-def own_kernel(k, v, sk, sv, own, kv):
-    kv[0] = sk[...]
-    kv[1] = sv[...]
+def own_kernel(k_far, v_far, sk_far, sv_far, own, kv, k, v, sem):
+    moves = [(k_far, k), (v_far, v), (sk_far, kv.at[0]), (sv_far, kv.at[1])]
+    copies = [pltpu.make_async_copy(a, b, sem.at[i]) for i, (a, b) in enumerate(moves)]
+    for copy in copies:
+        copy.start()
+    copies[0].wait()
+    copies[1].wait()
     for h in range(HERE):
         put_state(own, h, dot(head(k, h), head(v, h), 0, 0))
-
-
-def local_kernel(q, k, v, weights, local):
+    copies[2].wait()
+    copies[3].wait()
+
+
+def local_kernel(q_far, g_far, k, v, weights, local, q, g, sem):
+    moves = [(q_far, q), (g_far, g)]
+    copies = [pltpu.make_async_copy(a, b, sem.at[i]) for i, (a, b) in enumerate(moves)]
+    for copy in copies:
+        copy.start()
+    for copy in copies:
+        copy.wait()
     lower = lower_triangle()
     for h in range(HERE):
         w = jnp.where(lower, dot(head(q, h), head(k, h), 1, 1), 0.0).astype(bf16)
@@ -152,7 +170,8 @@
         part_v[:, at] = dot(weights[h], head(gm, h), 0, 0)
 
 
-def final_kernel(k, v, part_k, part_v, a, grad_k, grad_v):
+def final_kernel(k, v, part_k, part_v, a, after, grad_k, grad_v):
+    del after
     for h in range(HERE):
         at = slice(h * HD, (h + 1) * HD)
         later = state_of(a, h)
@@ -160,27 +179,39 @@
         grad_v[:, at] = (head(part_v, h) + dot(head(k, h), later, 1, 0)).astype(bf16)
 
 
-def soft_kernel(q, kv, doc_row, doc, out, qs, top, total, acc):
+def soft_kernel(q_far, kv_far, doc_row, doc, out, ended, q, kv, qs, top, total, acc, sem, kv_sem):
     me = lax.axis_index("ctx")
     my_y = me // NZ
     keys = CHUNK * T
     width = HERE * T
     factor = math.log2(math.e) / math.sqrt(HD)
+    first_chunk = doc[0] // keys
+    my_chunk = me // CHUNK
+    last_start = doc[T - 1]
+
+    def fetch(chunk):
+        block = chunk * CHUNK
+        source = kv_far.at[pl.ds(lax.rem(block, NZ), CHUNK), my_y - block // NZ]
+        return pltpu.make_async_copy(source, kv.at[chunk], kv_sem.at[chunk])
+
+    q_copy = pltpu.make_async_copy(q_far, q, sem)
+    q_copy.start()
+
+    def ask(chunk, carry):
+        fetch(chunk).start()
+        return carry
+
+    lax.fori_loop(first_chunk, my_chunk + 1, ask, 0)
+    q_copy.wait()
     for h in range(HERE):
         qs[h * T : (h + 1) * T] = head(q, h)
     top[...] = jnp.full((1, width), floor_score, f32)
     total[...] = jnp.zeros((1, width), f32)
     acc[...] = jnp.zeros((HD, width), f32)
-    first_chunk = doc[0] // keys
-    my_chunk = me // CHUNK
-    last_start = doc[T - 1]
 
     def visit(chunk, masked):
-        block = chunk * CHUNK
-        slot = my_y - block // NZ
-        z0 = lax.rem(block, NZ)
-        k = kv[pl.ds(z0, CHUNK), slot, 0].reshape(keys, HD)
-        v = kv[pl.ds(z0, CHUNK), slot, 1].reshape(keys, HD)
+        k = kv[chunk, :, 0].reshape(keys, HD)
+        v = kv[chunk, :, 1].reshape(keys, HD)
         scores = dot(k, qs[...], 1, 1)
         if masked:
             key_pos = chunk * keys + lax.broadcasted_iota(jnp.int32, (keys, width), 0)
@@ -199,6 +230,7 @@
         acc[...] = shrink * acc[...] + dot(v, probs.astype(bf16), 0, 0)
 
     def step(chunk, carry):
+        fetch(chunk).wait()
         clear = (chunk < my_chunk) & (chunk * keys >= last_start)
 
         @pl.when(clear)
@@ -212,32 +244,28 @@
         return carry
 
     lax.fori_loop(first_chunk, my_chunk + 1, step, 0)
+    ended[...] = jnp.zeros((8, HD), f32)
     result = acc[...] / total[...]
     for h in range(HERE):
         out[:, h * HD : (h + 1) * HD] = jnp.transpose(result[:, h * T : (h + 1) * T]).astype(bf16)
 
 
+def swap(pieces):
+    return lax.all_to_all(pieces, "ctx", 0, 0, tiled=True, axis_index_groups=z_groups)
+
+
 def carried_in(own, reverse):
-    pieces = (NZ, PIECE, HD)
     tag = "later" if reverse else "earlier"
-    swap = functools.partial(
-        lax.all_to_all,
-        axis_name="ctx",
-        split_axis=0,
-        concat_axis=0,
-        tiled=True,
-        axis_index_groups=z_groups,
-    )
     got = swap(own)
-    (line,) = call(total_kernel, [((PIECE, HD), bf16)], got, flops=1e5, name=tag + "_total")
+    (line,) = call(total_kernel, [((PIECE, HD), bf16)], got, flops=COST["total"], name=tag + "_total")
     sign = -1 if reverse else 1
     rows = [lax.ppermute(line, "ctx", y_shift(sign * s)) for s in (1, 2, 3)]
     (carried,) = call(
         functools.partial(carry_kernel, reverse),
-        [(pieces, bf16)],
+        [((NZ, PIECE, HD), bf16)],
         got,
         *rows,
-        flops=1e5,
+        flops=COST["carry"],
         name=tag + "_carry",
     )
     return swap(carried)
@@ -246,27 +274,39 @@
 def on_device(
     lin_query, lin_key, lin_value, lin_cotangent, soft_query, soft_key, soft_value, doc_start
 ):
-    q, k, v, g = lin_query, lin_key, lin_value, lin_cotangent
     wide = (T, HERE * HD)
     states = (NZ, PIECE, HD)
     squares = (HERE, T, T)
-    own, kv = call(
+    dma = pltpu.SemaphoreType.DMA
+    own, kv, k, v = call(
         own_kernel,
-        [(states, bf16), ((2, T, HD), bf16)],
+        [(states, bf16), ((2, T, HD), bf16), (wide, bf16), (wide, bf16)],
+        lin_key,
+        lin_value,
+        soft_key,
+        soft_value,
+        far=(0, 1, 2, 3),
+        flops=COST["own"],
+        vmem=BIG,
+        scratch=[dma((4,))],
+        name="own_state",
+    )
+    slots = [kv] + [lax.ppermute(kv, "ctx", y_shift(s)) for s in (1, 2, 3)]
+    all_kv = lax.all_gather(jnp.stack(slots), "ctx", axis_index_groups=z_groups)
+    weights, local, q, g = call(
+        local_kernel,
+        [(squares, bf16), (wide, f32), (wide, bf16), (wide, bf16)],
+        lin_query,
+        lin_cotangent,
         k,
         v,
-        soft_key,
-        soft_value,
-        name="own_state",
-    )
-    slots = [kv] + [lax.ppermute(kv, "ctx", y_shift(s)) for s in (1, 2, 3)]
-    all_kv = lax.all_gather(jnp.stack(slots), "ctx", axis_index_groups=z_groups)
-    weights, local = call(
-        local_kernel, [(squares, bf16), (wide, f32)], q, k, v, name="local"
+        far=(0, 1),
+        scratch=[dma((2,))],
+        flops=COST["local"], name="local",
     )
     earlier = carried_in(own, False)
     mix, sums = call(
-        mix_kernel, [(wide, f32), ((TP, 8, HD), f32)], q, g, local, earlier, name="mix"
+        mix_kernel, [(wide, f32), ((TP, 8, HD), f32)], q, g, local, earlier, flops=COST["mix"], name="mix"
     )
     sums = lax.all_to_all(sums, "tp", 0, 0, tiled=True)
     lin_out, gm, own_adjoint = call(
@@ -276,7 +316,7 @@
         g,
         mix,
         sums,
-        name="norm",
+        flops=COST["norm"], name="norm",
     )
     later = carried_in(own_adjoint, True)
     grad_query, part_k, part_v = call(
@@ -288,27 +328,33 @@
         gm,
         weights,
         earlier,
-        name="inside",
-    )
-    grad_key, grad_value = call(
-        final_kernel, [(wide, bf16), (wide, bf16)], k, v, part_k, part_v, later, name="final"
-    )
-    (soft_out,) = call(
+        flops=COST["inside"], name="inside",
+    )
+    soft_out, ended = call(
         soft_kernel,
-        [(wide, bf16)],
+        [(wide, bf16), ((8, HD), f32)],
         soft_query,
         all_kv,
         doc_start.reshape(1, T),
         doc_start,
         smem=(3,),
-        flops=1e9,
+        far=(0, 1),
+        flops=COST["soft"],
+        vmem=BIG,
         scratch=[
+            pltpu.VMEM(wide, bf16),
+            pltpu.VMEM((NY * NZ // CHUNK, CHUNK, 2, T, HD), bf16),
             pltpu.VMEM((HERE * T, HD), bf16),
             pltpu.VMEM((1, HERE * T), f32),
             pltpu.VMEM((1, HERE * T), f32),
             pltpu.VMEM((HD, HERE * T), f32),
+            dma,
+            dma((NY * NZ // CHUNK,)),
         ],
         name="soft",
+    )
+    grad_key, grad_value = call(
+        final_kernel, [(wide, bf16), (wide, bf16)], k, v, part_k, part_v, later, ended, far=(5,), flops=COST["final"], name="final"
     )
     return (lin_out, grad_query, grad_key, grad_value, soft_out)
 

time: 157 us -> 149 us (0.949)
  blocking collectives: 55.7 us -> 28.8 us
  starting transfers between devices: 24.5 us -> 44.1 us
  local copies, waits for them, and re-layouts: 11 us -> 0.71 us
  Pallas kernels: 14.2 us -> 19.6 us
  waiting for transfers between devices: 35.8 us -> 39.1 us
    all_to_all x2 -> x1, blocking collectives: 46.2 us -> 19.2 us  [swap(): lax.all_to_all(pieces, 'ctx', 0, 0, tiled=True, axis_index_groups=z_groups)]
    all_to_all x2 -> x3, starting transfers between devices: 8.13 us -> 28.1 us  [swap(): lax.all_to_all(pieces, 'ctx', 0, 0, tiled=True, axis_index_groups=z_groups)]
    all_gather x1, waiting for transfers between devices: 0.01 us -> 10.8 us  [on_device(): all_kv = lax.all_gather(jnp.stack(slots), 'ctx', axis_index_groups=z_groups)]
    unnamed x32 -> x10, local copies, waits for them, and re-layouts: 11 us -> 0.71 us
    all_to_all x2 -> x3, waiting for transfers between devices: 24.2 us -> 17.3 us  [swap(): lax.all_to_all(pieces, 'ctx', 0, 0, tiled=True, axis_index_groups=z_groups)]
    pallas_call x11, Pallas kernels: 14.2 us -> 19.6 us  [call(): pl.pallas_call(kernel, out_shape=[jax.ShapeDtypeStruct(s, d) for s, d in...]
  transfers between devices with their start and end apart: 12 -> 13, of which waited for: 6 -> 8; matrix products, arithmetic and copies ran while one was open for 0% -> 1% of each run, Pallas kernels for 4% -> 11%
where the time goes in v2:
time: 149 us; the launch traced here: 148 us
  starting transfers between devices  44.1 us (30%)
  waiting for transfers between devices  39.1 us (26%)
  blocking collectives  28.8 us (19%)
  Pallas kernels  19.6 us (13%)
  between operations  14.2 us (10%)
  other arithmetic  1.57 us (1%)
    all_to_all x3, starting transfers between devices, swap(): lax.all_to_all(pieces, 'ctx', 0, 0, tiled=True, axis_index_groups=z_groups)  28.1 us
    pallas_call x11, Pallas kernels, call(): pl.pallas_call(kernel, out_shape=[jax.ShapeDtypeStruct(s, d) for s, d in...  19.6 us
    all_to_all x1, blocking collectives, swap(): lax.all_to_all(pieces, 'ctx', 0, 0, tiled=True, axis_index_groups=z_groups)  19.2 us
    all_to_all x3, waiting for transfers between devices, swap(): lax.all_to_all(pieces, 'ctx', 0, 0, tiled=True, axis_index_groups=z_groups)  17.3 us
    ppermute x6, starting transfers between devices, carried_in(): rows = [lax.ppermute(line, 'ctx', y_shift(sign * s)) for s in (1, 2, 3)]  12.1 us
    all_gather x1, waiting for transfers between devices, on_device(): all_kv = lax.all_gather(jnp.stack(slots), 'ctx', axis_index_groups=z_groups)  10.8 us
    all_to_all x1, blocking collectives, on_device(): sums = lax.all_to_all(sums, 'tp', 0, 0, tiled=True)  9.56 us
    ppermute x6, waiting for transfers between devices, carried_in(): rows = [lax.ppermute(line, 'ctx', y_shift(sign * s)) for s in (1, 2, 3)]  5.79 us
  transfers between devices with their start and end apart: 13, of which 8 were waited for; matrix products, arithmetic and copies ran while one was open for 1% of the time, Pallas kernels for 11%

profile of v2, /device:TPU:24, one launch (start us, length us, event | category | flops | bytes accessed | tf_op | source)
XLA Modules:
  0.0 148.1 jit_solution(16848072399700885030)
XLA Ops:
  7.2 2.0 %own_state.1 = (bf16[16,32,128]{2,1,0:T(8,128)(2,1)}, bf16[2,128,128]{2,1,0:T(8,128)(2,1)}, bf16[128,512]{1,0:T(8,128)(2,1)}, bf16[128,512]{1,0:T(8,128)(2,1)}) custom-call(bf16[128,512]{1,0:T(8,128)(2,1)} %k_far.1, bf16[128,512]{1,0:T(8,128)(2,1)} %v_far.1, bf16[128,128]{1,0:T(8,128)(2,1)} %sk_far.1, bf16[128,128]{1,0:T(8,128)(2,1)} %sv_far.1), custom_call_target="tpu_custom_call" | custom-call | flops 100000000 | bytes 786432 | tf_op jit(solution)/shard_map/own_state/pallas_call | solution.py:51
  9.2 15.2 %all-to-all-start = ((bf16[16,32,128]{2,1,0:T(8,128)(2,1)}), bf16[16,32,128]{2,1,0:T(8,128)(2,1)S(1)}, u32[]{:S(2)}, u32[]{:S(2)}) async-start(bf16[16,32,128]{2,1,0:T(8,128)(2,1)} %get-tuple-element.30), calls=%async_computation | async-start | bytes 262144 | tf_op jit(solution)/shard_map/all_to_all | solution.py:254
  24.4 0.0 all-gather.3.cloned.1.call-start
  24.4 1.3 collective-permute-start.8
  25.7 1.3 collective-permute-start.7
  27.0 1.3 collective-permute-start.6
  28.3 4.4 %collective-permute-done.8 = bf16[2,128,128]{2,1,0:T(8,128)(2,1)S(1)} collective-permute-done((bf16[2,128,128]{2,1,0:T(8,128)(2,1)}, bf16[2,128,128]{2,1,0:T(8,128)(2,1)S(1)}, u32[]{:S(2)}, u32[]{:S(2)}) %collective-permute-start.8) | collective-permute-done | bytes 65568 | tf_op jit(solution)/shard_map/ppermute | solution.py:294
  32.7 0.9 collective-permute-done.7
  33.6 0.0 collective-permute-done.6
  33.6 1.6 %pad_maximum_fusion = bf16[4,2,128,128]{3,2,1,0:T(8,128)(2,1)} fusion(bf16[1,2,128,128]{3,2,1,0:T(8,128)(2,1)S(1)} %bitcast.8, bf16[1,2,128,128]{3,2,1,0:T(8,128)(2,1)S(1)} %bitcast.9, bf16[1,2,128,128]{3,2,1,0:T(8,128)(2,1)S(1)} %bitcast.10, bf16[1,2,128,128]{3,2,1,0:T(8,128)(2,1)} %bitcast.7), kind=kLoop, calls=%fused_computation | loop fusion | flops 393216 | bytes 524288 | tf_op jit(solution)/shard_map/stack | solution.py:295
  35.2 0.0 all-gather.3.cloned.1.call-update
  35.2 3.9 %all-to-all-done.r = bf16[16,32,128]{2,1,0:T(8,128)(2,1)S(1)} async-done(((bf16[16,32,128]{2,1,0:T(8,128)(2,1)}), bf16[16,32,128]{2,1,0:T(8,128)(2,1)S(1)}, u32[]{:S(2)}, u32[]{:S(2)}) %all-to-all-start) | async-done | bytes 131104 | tf_op jit(solution)/shard_map/all_to_all | solution.py:254
  39.1 0.0 copy-start
  39.1 0.0 copy-start.1
  39.1 0.0 copy-start.2
  39.1 0.0 copy-start.3
  39.1 1.4 collective-permute-start.2
  40.6 1.3 collective-permute-start.1
  41.9 1.3 collective-permute-start
  43.2 2.9 %collective-permute-done.2.c = bf16[32,128]{1,0:T(8,128)(2,1)S(1)} collective-permute-done((bf16[32,128]{1,0:T(8,128)(2,1)S(1)}, bf16[32,128]{1,0:T(8,128)(2,1)S(1)}, u32[]{:S(2)}, u32[]{:S(2)}) %collective-permute-start.2) | collective-permute-done | bytes 8224 | tf_op jit(solution)/shard_map/ppermute | solution.py:262
  46.0 1.6 %collective-permute-done.1.b = bf16[32,128]{1,0:T(8,128)(2,1)S(1)} collective-permute-done((bf16[32,128]{1,0:T(8,128)(2,1)S(1)}, bf16[32,128]{1,0:T(8,128)(2,1)S(1)}, u32[]{:S(2)}, u32[]{:S(2)}) %collective-permute-start.1) | collective-permute-done | bytes 8224 | tf_op jit(solution)/shard_map/ppermute | solution.py:262
  47.6 0.0 collective-permute-done.a
  47.6 0.7 earlier_carry.1
  48.3 8.2 %all-to-all-start.1 = ((bf16[16,32,128]{2,1,0:T(8,128)(2,1)}), bf16[16,32,128]{2,1,0:T(8,128)(2,1)S(1)}, u32[]{:S(2)}, u32[]{:S(2)}) async-start(bf16[16,32,128]{2,1,0:T(8,128)(2,1)} %earlier_carry.1), calls=%async_computation.1 | async-start | bytes 262144 | tf_op jit(solution)/shard_map/all_to_all | solution.py:254
  56.5 0.0 copy-done
  56.5 0.0 copy-done.1
  56.5 0.0 copy-done.2
  56.5 0.0 copy-done.3
  56.5 1.1 local.1
  57.6 13.4 %all-to-all-done.1.s = bf16[16,32,128]{2,1,0:T(8,128)(2,1)S(1)} async-done(((bf16[16,32,128]{2,1,0:T(8,128)(2,1)}), bf16[16,32,128]{2,1,0:T(8,128)(2,1)S(1)}, u32[]{:S(2)}, u32[]{:S(2)}) %all-to-all-start.1) | async-done | bytes 131104 | tf_op jit(solution)/shard_map/all_to_all | solution.py:254
  71.0 0.3 mix.1
  71.3 9.6 %all_to_all.25.sums = f32[8,8,128]{2,1,0:T(8,128)S(1)} all-to-all(f32[8,8,128]{2,1,0:T(8,128)S(1)} %get-tuple-element.32), channel_id=1, replica_groups=mesh['ctx'=64,'tp'=8] {'tp'}, dimensions={0} | all-to-all | bytes 65536 | tf_op jit(solution)/shard_map/all_to_all | solution.py:311
  80.9 0.9 norm.1
  81.8 19.2 %all_to_all.26.r = bf16[16,32,128]{2,1,0:T(8,128)(2,1)S(1)} all-to-all(bf16[16,32,128]{2,1,0:T(8,128)(2,1)S(1)} %get-tuple-element.39), channel_id=1, replica_groups={{0,8,16,24,32,40,48,56,64,72,80,88,96,104,112,120},{128,136,144,152,160..., dimensions={0} | all-to-all | bytes 262144 | tf_op jit(solution)/shard_map/all_to_all | solution.py:254
  101.1 4.0 %collective-permute-start.5 = (bf16[32,128]{1,0:T(8,128)(2,1)S(1)}, bf16[32,128]{1,0:T(8,128)(2,1)S(1)}, u32[]{:S(2)}, u32[]{:S(2)}) collective-permute-start(bf16[32,128]{1,0:T(8,128)(2,1)S(1)} %later_total.1), channel_id=1, source_target_pairs={{384,0},{392,8},{400,16},{408,24},{416,32},{424,40},{432,48},{440,... | collective-permute-start | bytes 24584 | tf_op jit(solution)/shard_map/ppermute | solution.py:262
  105.0 2.8 %collective-permute-start.4 = (bf16[32,128]{1,0:T(8,128)(2,1)S(1)}, bf16[32,128]{1,0:T(8,128)(2,1)S(1)}, u32[]{:S(2)}, u32[]{:S(2)}) collective-permute-start(bf16[32,128]{1,0:T(8,128)(2,1)S(1)} %later_total.1), channel_id=1, source_target_pairs={{256,0},{264,8},{272,16},{280,24},{288,32},{296,40},{304,48},{312,... | collective-permute-start | bytes 24584 | tf_op jit(solution)/shard_map/ppermute | solution.py:262
  107.9 1.3 collective-permute-start.3
  109.2 0.0 collective-permute-done.5.c
  109.2 0.0 collective-permute-done.4.b
  109.2 1.3 collective-permute-done.3.a
  110.5 0.7 later_carry.1
  111.2 4.7 %all-to-all-start.4 = ((bf16[16,32,128]{2,1,0:T(8,128)(2,1)}), bf16[16,32,128]{2,1,0:T(8,128)(2,1)S(1)}, u32[]{:S(2)}, u32[]{:S(2)}) async-start(bf16[16,32,128]{2,1,0:T(8,128)(2,1)} %later_carry.1), calls=%async_computation.4 | async-start | bytes 262144 | tf_op jit(solution)/shard_map/all_to_all | solution.py:254
  115.9 1.4 inside.1
  117.3 10.8 %all-gather.3.cloned.1.call-done = bf16[64,2,128,128]{3,2,1,0:T(8,128)(2,1)} async-done(((bf16[4,2,128,128]{3,2,1,0:T(8,128)(2,1)}), bf16[64,2,128,128]{3,2,1,0:T(8,128)(2,1)}) %all-gather.3.cloned.1.call-update) | async-done | bytes 4194320 | tf_op jit(solution)/shard_map/all_gather | solution.py:295
  128.1 11.5 %soft.1 = (bf16[128,512]{1,0:T(8,128)(2,1)}, f32[8,128]{1,0:T(8,128)}) custom-call(bf16[128,512]{1,0:T(8,128)(2,1)} %q_far.3, bf16[16,4,2,128,128]{4,3,2,1,0:T(8,128)(2,1)} %bitcast.6, s32[1,128]{1,0:T(1,128)} %bitcast.11, s32[128]{0:T(128)} %doc.1), custom_call_target="tpu_custom_call" | custom-call | flops 100000000 | bytes 4461568 | tf_op jit(solution)/shard_map/soft/pallas_call | solution.py:51
  139.6 0.0 all-to-all-done.4.a
  139.6 0.0 copy-start.4
  139.6 0.7 copy-done.4
  140.3 0.9 final.1
  (2 shorter events, 0.0 us)
Async XLA Ops:
  9.2 29.9 %all-to-all-start = ((bf16[16,32,128]{2,1,0:T(8,128)(2,1)}), bf16[16,32,128]{2,1,0:T(8,128)(2,1)S(1)}, u32[]{:S(2)}, u32[]{:S(2)}) async-start(bf16[16,32,128]{2,1,0:T(8,128)(2,1)} %get-tuple-element.30), calls=%async_computation | async-start | bytes 262144 | tf_op jit(solution)/shard_map/all_to_all | solution.py:254
  24.4 103.7 %all-gather.3.cloned.1.call-start = ((), (), s32[]{:S(2)}) async-start(), calls=%async_computation.5 | async-start | bytes 4456448 | tf_op jit(solution)/shard_map/all_gather | solution.py:295
  24.4 8.3 %collective-permute-start.8 = (bf16[2,128,128]{2,1,0:T(8,128)(2,1)}, bf16[2,128,128]{2,1,0:T(8,128)(2,1)S(1)}, u32[]{:S(2)}, u32[]{:S(2)}) collective-permute-start(bf16[2,128,128]{2,1,0:T(8,128)(2,1)} %get-tuple-element.40), channel_id=1, source_target_pairs={{0,384},{8,392},{16,400},{24,408},{32,416},{40,424},{48,432},{56,4... | collective-permute-start | bytes 196616 | tf_op jit(solution)/shard_map/ppermute | solution.py:294
  25.7 7.9 %collective-permute-start.7 = (bf16[2,128,128]{2,1,0:T(8,128)(2,1)}, bf16[2,128,128]{2,1,0:T(8,128)(2,1)S(1)}, u32[]{:S(2)}, u32[]{:S(2)}) collective-permute-start(bf16[2,128,128]{2,1,0:T(8,128)(2,1)} %get-tuple-element.40), channel_id=1, source_target_pairs={{0,256},{8,264},{16,272},{24,280},{32,288},{40,296},{48,304},{56,3... | collective-permute-start | bytes 196616 | tf_op jit(solution)/shard_map/ppermute | solution.py:294
  27.0 6.6 %collective-permute-start.6 = (bf16[2,128,128]{2,1,0:T(8,128)(2,1)}, bf16[2,128,128]{2,1,0:T(8,128)(2,1)S(1)}, u32[]{:S(2)}, u32[]{:S(2)}) collective-permute-start(bf16[2,128,128]{2,1,0:T(8,128)(2,1)} %get-tuple-element.40), channel_id=1, source_target_pairs={{0,128},{8,136},{16,144},{24,152},{32,160},{40,168},{48,176},{56,1... | collective-permute-start | bytes 196616 | tf_op jit(solution)/shard_map/ppermute | solution.py:294
  39.1 17.4 %copy-start = (bf16[128,512]{1,0:T(8,128)(2,1)S(1)}, bf16[128,512]{1,0:T(8,128)(2,1)}, u32[]{:S(2)}) copy-start(bf16[128,512]{1,0:T(8,128)(2,1)} %get-tuple-element.25.k) | copy-start | bytes 393220
  39.1 17.4 %copy-start.1 = (bf16[128,512]{1,0:T(8,128)(2,1)S(1)}, bf16[128,512]{1,0:T(8,128)(2,1)}, u32[]{:S(2)}) copy-start(bf16[128,512]{1,0:T(8,128)(2,1)} %get-tuple-element.26.v) | copy-start | bytes 393220
  39.1 17.4 %copy-start.2 = (bf16[128,512]{1,0:T(8,128)(2,1)S(1)}, bf16[128,512]{1,0:T(8,128)(2,1)}, u32[]{:S(2)}) copy-start(bf16[128,512]{1,0:T(8,128)(2,1)} %q_far.2) | copy-start | bytes 393220
  39.1 17.4 %copy-start.3 = (bf16[128,512]{1,0:T(8,128)(2,1)S(1)}, bf16[128,512]{1,0:T(8,128)(2,1)}, u32[]{:S(2)}) copy-start(bf16[128,512]{1,0:T(8,128)(2,1)} %g_far.1) | copy-start | bytes 393220
  39.1 6.9 %collective-permute-start.2 = (bf16[32,128]{1,0:T(8,128)(2,1)S(1)}, bf16[32,128]{1,0:T(8,128)(2,1)S(1)}, u32[]{:S(2)}, u32[]{:S(2)}) collective-permute-start(bf16[32,128]{1,0:T(8,128)(2,1)S(1)} %earlier_total.1), channel_id=1, source_target_pairs={{0,384},{8,392},{16,400},{24,408},{32,416},{40,424},{48,432},{56,4... | collective-permute-start | bytes 24584 | tf_op jit(solution)/shard_map/ppermute | solution.py:262
  40.6 7.0 %collective-permute-start.1 = (bf16[32,128]{1,0:T(8,128)(2,1)S(1)}, bf16[32,128]{1,0:T(8,128)(2,1)S(1)}, u32[]{:S(2)}, u32[]{:S(2)}) collective-permute-start(bf16[32,128]{1,0:T(8,128)(2,1)S(1)} %earlier_total.1), channel_id=1, source_target_pairs={{0,256},{8,264},{16,272},{24,280},{32,288},{40,296},{48,304},{56,3... | collective-permute-start | bytes 24584 | tf_op jit(solution)/shard_map/ppermute | solution.py:262
  41.9 5.8 %collective-permute-start = (bf16[32,128]{1,0:T(8,128)(2,1)S(1)}, bf16[32,128]{1,0:T(8,128)(2,1)S(1)}, u32[]{:S(2)}, u32[]{:S(2)}) collective-permute-start(bf16[32,128]{1,0:T(8,128)(2,1)S(1)} %earlier_total.1), channel_id=1, source_target_pairs={{0,128},{8,136},{16,144},{24,152},{32,160},{40,168},{48,176},{56,1... | collective-permute-start | bytes 24584 | tf_op jit(solution)/shard_map/ppermute | solution.py:262
  48.3 22.7 %all-to-all-start.1 = ((bf16[16,32,128]{2,1,0:T(8,128)(2,1)}), bf16[16,32,128]{2,1,0:T(8,128)(2,1)S(1)}, u32[]{:S(2)}, u32[]{:S(2)}) async-start(bf16[16,32,128]{2,1,0:T(8,128)(2,1)} %earlier_carry.1), calls=%async_computation.1 | async-start | bytes 262144 | tf_op jit(solution)/shard_map/all_to_all | solution.py:254
  101.1 8.1 %collective-permute-start.5 = (bf16[32,128]{1,0:T(8,128)(2,1)S(1)}, bf16[32,128]{1,0:T(8,128)(2,1)S(1)}, u32[]{:S(2)}, u32[]{:S(2)}) collective-permute-start(bf16[32,128]{1,0:T(8,128)(2,1)S(1)} %later_total.1), channel_id=1, source_target_pairs={{384,0},{392,8},{400,16},{408,24},{416,32},{424,40},{432,48},{440,... | collective-permute-start | bytes 24584 | tf_op jit(solution)/shard_map/ppermute | solution.py:262
  105.0 4.2 %collective-permute-start.4 = (bf16[32,128]{1,0:T(8,128)(2,1)S(1)}, bf16[32,128]{1,0:T(8,128)(2,1)S(1)}, u32[]{:S(2)}, u32[]{:S(2)}) collective-permute-start(bf16[32,128]{1,0:T(8,128)(2,1)S(1)} %later_total.1), channel_id=1, source_target_pairs={{256,0},{264,8},{272,16},{280,24},{288,32},{296,40},{304,48},{312,... | collective-permute-start | bytes 24584 | tf_op jit(solution)/shard_map/ppermute | solution.py:262
  107.9 2.6 %collective-permute-start.3 = (bf16[32,128]{1,0:T(8,128)(2,1)S(1)}, bf16[32,128]{1,0:T(8,128)(2,1)S(1)}, u32[]{:S(2)}, u32[]{:S(2)}) collective-permute-start(bf16[32,128]{1,0:T(8,128)(2,1)S(1)} %later_total.1), channel_id=1, source_target_pairs={{128,0},{136,8},{144,16},{152,24},{160,32},{168,40},{176,48},{184,... | collective-permute-start | bytes 24584 | tf_op jit(solution)/shard_map/ppermute | solution.py:262
  111.2 28.4 %all-to-all-start.4 = ((bf16[16,32,128]{2,1,0:T(8,128)(2,1)}), bf16[16,32,128]{2,1,0:T(8,128)(2,1)S(1)}, u32[]{:S(2)}, u32[]{:S(2)}) async-start(bf16[16,32,128]{2,1,0:T(8,128)(2,1)} %later_carry.1), calls=%async_computation.4 | async-start | bytes 262144 | tf_op jit(solution)/shard_map/all_to_all | solution.py:254
  139.6 0.7 copy-start.4
Sparse Core Ops, SparseCore 0:
  35.3 92.7 all-gather.2

commit v3 on v2

--- a/solution.py
+++ b/solution.py
@@ -21,13 +21,14 @@
 CHUNK = 4
 
 BIG = 60 * 2**20
-COST = dict(own=1e8, local=1e8, total=1e10, carry=1e10, mix=1.6e10, norm=1.6e10, inside=1e8, final=1e8, soft=1e8)
+COST = dict(own=1e8, local=1e8, total=1e5, carry=1e5, mix=1e8, norm=1e8, inside=1e8, final=1e8, soft=1e8)
 
 epsilon = 1e-06
 floor_score = -1e30
 bf16 = jnp.bfloat16
 f32 = jnp.float32
 
+y_groups = [[y * NZ + z for y in range(NY)] for z in range(NZ)]
 z_groups = [[y * NZ + z for z in range(NZ)] for y in range(NY)]
 
 
@@ -85,7 +86,7 @@
 
 
 def own_kernel(k_far, v_far, sk_far, sv_far, own, kv, k, v, sem):
-    moves = [(k_far, k), (v_far, v), (sk_far, kv.at[0]), (sv_far, kv.at[1])]
+    moves = [(k_far, k), (v_far, v), (sk_far, kv.at[0, 0]), (sv_far, kv.at[0, 1])]
     copies = [pltpu.make_async_copy(a, b, sem.at[i]) for i, (a, b) in enumerate(moves)]
     for copy in copies:
         copy.start()
@@ -95,6 +96,8 @@
         put_state(own, h, dot(head(k, h), head(v, h), 0, 0))
     copies[2].wait()
     copies[3].wait()
+    for y in range(1, NY):
+        kv[y] = kv[0]
 
 
 def local_kernel(q_far, g_far, k, v, weights, local, q, g, sem):
@@ -181,7 +184,6 @@
 
 def soft_kernel(q_far, kv_far, doc_row, doc, out, ended, q, kv, qs, top, total, acc, sem, kv_sem):
     me = lax.axis_index("ctx")
-    my_y = me // NZ
     keys = CHUNK * T
     width = HERE * T
     factor = math.log2(math.e) / math.sqrt(HD)
@@ -191,7 +193,7 @@
 
     def fetch(chunk):
         block = chunk * CHUNK
-        source = kv_far.at[pl.ds(lax.rem(block, NZ), CHUNK), my_y - block // NZ]
+        source = kv_far.at[pl.ds(lax.rem(block, NZ), CHUNK), block // NZ]
         return pltpu.make_async_copy(source, kv.at[chunk], kv_sem.at[chunk])
 
     q_copy = pltpu.make_async_copy(q_far, q, sem)
@@ -280,7 +282,7 @@
     dma = pltpu.SemaphoreType.DMA
     own, kv, k, v = call(
         own_kernel,
-        [(states, bf16), ((2, T, HD), bf16), (wide, bf16), (wide, bf16)],
+        [(states, bf16), ((NY, 2, T, HD), bf16), (wide, bf16), (wide, bf16)],
         lin_key,
         lin_value,
         soft_key,
@@ -291,8 +293,8 @@
         scratch=[dma((4,))],
         name="own_state",
     )
-    slots = [kv] + [lax.ppermute(kv, "ctx", y_shift(s)) for s in (1, 2, 3)]
-    all_kv = lax.all_gather(jnp.stack(slots), "ctx", axis_index_groups=z_groups)
+    line_kv = lax.all_to_all(kv, "ctx", 0, 0, tiled=True, axis_index_groups=y_groups)
+    all_kv = lax.all_gather(line_kv, "ctx", axis_index_groups=z_groups)
     weights, local, q, g = call(
         local_kernel,
         [(squares, bf16), (wide, f32), (wide, bf16), (wide, bf16)],

time: 149 us -> 144 us (0.966)
  blocking collectives: 28.8 us -> 67.2 us
  starting transfers between devices: 44.1 us -> 20.5 us
  waiting for transfers between devices: 39.1 us -> 16.1 us
  local copies, waits for them, and re-layouts: 0.71 us -> 4.31 us
  other arithmetic: 1.57 us -> 0 us
    all_to_all x1 -> x2, blocking collectives: 19.2 us -> 43.4 us  [swap(): lax.all_to_all(pieces, 'ctx', 0, 0, tiled=True, axis_index_groups=z_groups)]
    all_to_all x3 -> x2, starting transfers between devices: 28.1 us -> 9.1 us  [swap(): lax.all_to_all(pieces, 'ctx', 0, 0, tiled=True, axis_index_groups=z_groups)]
    all_to_all x0 -> x1, blocking collectives: none -> 14.5 us  [on_device(): lax.all_to_all(kv, 'ctx', 0, 0, tiled=True, axis_index_groups=y_groups)]
    all_gather x1, waiting for transfers between devices: 10.8 us -> 0.01 us  [on_device(): all_kv = lax.all_gather(line_kv, 'ctx', axis_index_groups=z_groups)]
    all_to_all x3 -> x2, waiting for transfers between devices: 17.3 us -> 10.3 us  [swap(): lax.all_to_all(pieces, 'ctx', 0, 0, tiled=True, axis_index_groups=z_groups)]
    ppermute x3 -> x0, waiting for transfers between devices: 5.28 us -> none  [on_device(): slots = [kv] + [lax.ppermute(kv, 'ctx', y_shift(s)) for s in (1, 2, 3)]]
    ppermute x3 -> x0, starting transfers between devices: 3.88 us -> none  [on_device(): slots = [kv] + [lax.ppermute(kv, 'ctx', y_shift(s)) for s in (1, 2, 3)]]
    unnamed x10 -> x14, local copies, waits for them, and re-layouts: 0.71 us -> 4.31 us
  transfers between devices with their start and end apart: 13 -> 9, of which waited for: 8 -> 5; matrix products, arithmetic and copies ran while one was open for 1% -> 0% of each run, Pallas kernels for 11% -> 12%
where the time goes in v3:
time: 144 us; the launch traced here: 142 us
  blocking collectives  67.2 us (47%)
  starting transfers between devices  20.5 us (14%)
  Pallas kernels  19.6 us (14%)
  waiting for transfers between devices  16.1 us (11%)
  between operations  14.2 us (10%)
  local copies, waits for them, and re-layouts  4.31 us (3%)
    all_to_all x2, blocking collectives, swap(): lax.all_to_all(pieces, 'ctx', 0, 0, tiled=True, axis_index_groups=z_groups)  43.4 us
    pallas_call x11, Pallas kernels, call(): pl.pallas_call(kernel, out_shape=[jax.ShapeDtypeStruct(s, d) for s, d in...  19.6 us
    all_to_all x1, blocking collectives, on_device(): lax.all_to_all(kv, 'ctx', 0, 0, tiled=True, axis_index_groups=y_groups)  14.5 us
    ppermute x6, starting transfers between devices, carried_in(): rows = [lax.ppermute(line, 'ctx', y_shift(sign * s)) for s in (1, 2, 3)]  11.3 us
    all_to_all x2, waiting for transfers between devices, swap(): lax.all_to_all(pieces, 'ctx', 0, 0, tiled=True, axis_index_groups=z_groups)  10.3 us
    all_to_all x1, blocking collectives, on_device(): sums = lax.all_to_all(sums, 'tp', 0, 0, tiled=True)  9.35 us
    all_to_all x2, starting transfers between devices, swap(): lax.all_to_all(pieces, 'ctx', 0, 0, tiled=True, axis_index_groups=z_groups)  9.1 us
    ppermute x6, waiting for transfers between devices, carried_in(): rows = [lax.ppermute(line, 'ctx', y_shift(sign * s)) for s in (1, 2, 3)]  5.78 us
  transfers between devices with their start and end apart: 9, of which 5 were waited for; matrix products, arithmetic and copies ran while one was open for 0% of the time, Pallas kernels for 12%

profile of v3, /device:TPU:24, one launch (start us, length us, event | category | flops | bytes accessed | tf_op | source)
XLA Modules:
  0.0 142.0 jit_solution(7026212272722837268)
XLA Ops:
  7.2 0.0 all-gather.3.cloned.1.call-start
  7.2 2.0 %own_state.1 = (bf16[16,32,128]{2,1,0:T(8,128)(2,1)}, bf16[4,2,128,128]{3,2,1,0:T(8,128)(2,1)}, bf16[128,512]{1,0:T(8,128)(2,1)}, bf16[128,512]{1,0:T(8,128)(2,1)}) custom-call(bf16[128,512]{1,0:T(8,128)(2,1)} %k_far.1, bf16[128,512]{1,0:T(8,128)(2,1)} %v_far.1, bf16[128,128]{1,0:T(8,128)(2,1)} %sk_far.1, bf16[128,128]{1,0:T(8,128)(2,1)} %sv_far.1), custom_call_target="tpu_custom_call" | custom-call | flops 100000000 | bytes 983040 | tf_op jit(solution)/shard_map/own_state/pallas_call | solution.py:52
  9.3 0.0 copy-start.1
  9.3 0.0 copy-start.3
  9.3 14.5 %all_to_all.30 = bf16[4,2,128,128]{3,2,1,0:T(8,128)(2,1)} all-to-all(bf16[4,2,128,128]{3,2,1,0:T(8,128)(2,1)} %get-tuple-element.40), channel_id=1, replica_groups={{0,128,256,384},{8,136,264,392},{16,144,272,400},{24,152,280,408},{32,1..., dimensions={0} | all-to-all | bytes 524288 | tf_op jit(solution)/shard_map/all_to_all | solution.py:296
  23.8 0.0 all-gather.3.cloned.1.call-update
  23.8 23.7 %all_to_all.31.r = bf16[16,32,128]{2,1,0:T(8,128)(2,1)S(1)} all-to-all(bf16[16,32,128]{2,1,0:T(8,128)(2,1)} %get-tuple-element.30), channel_id=1, replica_groups={{0,8,16,24,32,40,48,56,64,72,80,88,96,104,112,120},{128,136,144,152,160..., dimensions={0} | all-to-all | bytes 262144 | tf_op jit(solution)/shard_map/all_to_all | solution.py:256
  47.6 1.3 collective-permute-start.2
  48.9 1.3 collective-permute-start.1
  50.2 1.3 collective-permute-start
  51.5 2.9 %collective-permute-done.2.c = bf16[32,128]{1,0:T(8,128)(2,1)S(1)} collective-permute-done((bf16[32,128]{1,0:T(8,128)(2,1)S(1)}, bf16[32,128]{1,0:T(8,128)(2,1)S(1)}, u32[]{:S(2)}, u32[]{:S(2)}) %collective-permute-start.2) | collective-permute-done | bytes 8224 | tf_op jit(solution)/shard_map/ppermute | solution.py:264
  54.3 1.6 %collective-permute-done.1.b = bf16[32,128]{1,0:T(8,128)(2,1)S(1)} collective-permute-done((bf16[32,128]{1,0:T(8,128)(2,1)S(1)}, bf16[32,128]{1,0:T(8,128)(2,1)S(1)}, u32[]{:S(2)}, u32[]{:S(2)}) %collective-permute-start.1) | collective-permute-done | bytes 8224 | tf_op jit(solution)/shard_map/ppermute | solution.py:264
  55.9 0.0 collective-permute-done.a
  55.9 0.7 earlier_carry.1
  56.6 3.8 %all-to-all-start.1 = ((bf16[16,32,128]{2,1,0:T(8,128)(2,1)}), bf16[16,32,128]{2,1,0:T(8,128)(2,1)S(1)}, u32[]{:S(2)}, u32[]{:S(2)}) async-start(bf16[16,32,128]{2,1,0:T(8,128)(2,1)} %earlier_carry.1), calls=%async_computation.1 | async-start | bytes 262144 | tf_op jit(solution)/shard_map/all_to_all | solution.py:256
  60.4 0.0 copy-start
  60.4 0.9 copy-done
  61.3 0.0 copy-start.2
  61.3 0.9 copy-done.2
  62.2 0.0 copy-start.4
  62.2 0.9 copy-done.4
  63.1 0.0 copy-start.5
  63.1 0.9 copy-done.5
  64.0 1.1 local.1
  65.1 9.5 %all-to-all-done.1.s = bf16[16,32,128]{2,1,0:T(8,128)(2,1)S(1)} async-done(((bf16[16,32,128]{2,1,0:T(8,128)(2,1)}), bf16[16,32,128]{2,1,0:T(8,128)(2,1)S(1)}, u32[]{:S(2)}, u32[]{:S(2)}) %all-to-all-start.1) | async-done | bytes 131104 | tf_op jit(solution)/shard_map/all_to_all | solution.py:256
  74.6 0.3 mix.1
  74.9 9.3 %all_to_all.32.sums = f32[8,8,128]{2,1,0:T(8,128)S(1)} all-to-all(f32[8,8,128]{2,1,0:T(8,128)S(1)} %get-tuple-element.32), channel_id=1, replica_groups=mesh['ctx'=64,'tp'=8] {'tp'}, dimensions={0} | all-to-all | bytes 65536 | tf_op jit(solution)/shard_map/all_to_all | solution.py:313
  84.2 0.9 norm.1
  85.1 19.7 %all_to_all.33.r = bf16[16,32,128]{2,1,0:T(8,128)(2,1)S(1)} all-to-all(bf16[16,32,128]{2,1,0:T(8,128)(2,1)S(1)} %get-tuple-element.39), channel_id=1, replica_groups={{0,8,16,24,32,40,48,56,64,72,80,88,96,104,112,120},{128,136,144,152,160..., dimensions={0} | all-to-all | bytes 262144 | tf_op jit(solution)/shard_map/all_to_all | solution.py:256
  104.8 3.4 %collective-permute-start.5 = (bf16[32,128]{1,0:T(8,128)(2,1)S(1)}, bf16[32,128]{1,0:T(8,128)(2,1)S(1)}, u32[]{:S(2)}, u32[]{:S(2)}) collective-permute-start(bf16[32,128]{1,0:T(8,128)(2,1)S(1)} %later_total.1), channel_id=1, source_target_pairs={{384,0},{392,8},{400,16},{408,24},{416,32},{424,40},{432,48},{440,... | collective-permute-start | bytes 24584 | tf_op jit(solution)/shard_map/ppermute | solution.py:264
  108.3 2.6 %collective-permute-start.4 = (bf16[32,128]{1,0:T(8,128)(2,1)S(1)}, bf16[32,128]{1,0:T(8,128)(2,1)S(1)}, u32[]{:S(2)}, u32[]{:S(2)}) collective-permute-start(bf16[32,128]{1,0:T(8,128)(2,1)S(1)} %later_total.1), channel_id=1, source_target_pairs={{256,0},{264,8},{272,16},{280,24},{288,32},{296,40},{304,48},{312,... | collective-permute-start | bytes 24584 | tf_op jit(solution)/shard_map/ppermute | solution.py:264
  110.9 1.4 %collective-permute-start.3 = (bf16[32,128]{1,0:T(8,128)(2,1)S(1)}, bf16[32,128]{1,0:T(8,128)(2,1)S(1)}, u32[]{:S(2)}, u32[]{:S(2)}) collective-permute-start(bf16[32,128]{1,0:T(8,128)(2,1)S(1)} %later_total.1), channel_id=1, source_target_pairs={{128,0},{136,8},{144,16},{152,24},{160,32},{168,40},{176,48},{184,... | collective-permute-start | bytes 24584 | tf_op jit(solution)/shard_map/ppermute | solution.py:264
  112.3 0.0 collective-permute-done.5.c
  112.3 0.0 collective-permute-done.4.b
  112.3 1.3 collective-permute-done.3.a
  113.7 0.7 later_carry.1
  114.4 5.3 %all-to-all-start.4 = ((bf16[16,32,128]{2,1,0:T(8,128)(2,1)}), bf16[16,32,128]{2,1,0:T(8,128)(2,1)S(1)}, u32[]{:S(2)}, u32[]{:S(2)}) async-start(bf16[16,32,128]{2,1,0:T(8,128)(2,1)} %later_carry.1), calls=%async_computation.4 | async-start | bytes 262144 | tf_op jit(solution)/shard_map/all_to_all | solution.py:256
  119.7 0.0 copy-done.1
  119.7 0.0 copy-done.3
  119.7 1.4 inside.1
  121.1 0.0 all-gather.3.cloned.1.call-done
  121.1 11.5 %soft.1 = (bf16[128,512]{1,0:T(8,128)(2,1)}, f32[8,128]{1,0:T(8,128)}) custom-call(bf16[128,512]{1,0:T(8,128)(2,1)} %q_far.3, bf16[16,4,2,128,128]{4,3,2,1,0:T(8,128)(2,1)} %bitcast.2, s32[1,128]{1,0:T(1,128)} %bitcast.3, s32[128]{0:T(128)} %doc.1), custom_call_target="tpu_custom_call" | custom-call | flops 100000000 | bytes 4461568 | tf_op jit(solution)/shard_map/soft/pallas_call | solution.py:52
  132.6 0.9 all-to-all-done.4.a
  133.5 0.0 copy-start.6
  133.5 0.7 copy-done.6
  134.2 0.9 final.1
  (2 shorter events, 0.0 us)
Async XLA Ops:
  7.2 113.9 %all-gather.3.cloned.1.call-start = ((), (), s32[]{:S(2)}) async-start(), calls=%async_computation.6 | async-start | bytes 4456448 | tf_op jit(solution)/shard_map/all_gather | solution.py:297
  9.3 110.4 %copy-start.1 = (bf16[128,512]{1,0:T(8,128)(2,1)S(1)}, bf16[128,512]{1,0:T(8,128)(2,1)}, u32[]{:S(2)}) copy-start(bf16[128,512]{1,0:T(8,128)(2,1)} %get-tuple-element.25.k) | copy-start | bytes 393220
  9.3 110.4 %copy-start.3 = (bf16[128,512]{1,0:T(8,128)(2,1)S(1)}, bf16[128,512]{1,0:T(8,128)(2,1)}, u32[]{:S(2)}) copy-start(bf16[128,512]{1,0:T(8,128)(2,1)} %get-tuple-element.26.v) | copy-start | bytes 393220
  47.6 6.8 %collective-permute-start.2 = (bf16[32,128]{1,0:T(8,128)(2,1)S(1)}, bf16[32,128]{1,0:T(8,128)(2,1)S(1)}, u32[]{:S(2)}, u32[]{:S(2)}) collective-permute-start(bf16[32,128]{1,0:T(8,128)(2,1)S(1)} %earlier_total.1), channel_id=1, source_target_pairs={{0,384},{8,392},{16,400},{24,408},{32,416},{40,424},{48,432},{56,4... | collective-permute-start | bytes 24584 | tf_op jit(solution)/shard_map/ppermute | solution.py:264
  48.9 7.0 %collective-permute-start.1 = (bf16[32,128]{1,0:T(8,128)(2,1)S(1)}, bf16[32,128]{1,0:T(8,128)(2,1)S(1)}, u32[]{:S(2)}, u32[]{:S(2)}) collective-permute-start(bf16[32,128]{1,0:T(8,128)(2,1)S(1)} %earlier_total.1), channel_id=1, source_target_pairs={{0,256},{8,264},{16,272},{24,280},{32,288},{40,296},{48,304},{56,3... | collective-permute-start | bytes 24584 | tf_op jit(solution)/shard_map/ppermute | solution.py:264
  50.2 5.8 %collective-permute-start = (bf16[32,128]{1,0:T(8,128)(2,1)S(1)}, bf16[32,128]{1,0:T(8,128)(2,1)S(1)}, u32[]{:S(2)}, u32[]{:S(2)}) collective-permute-start(bf16[32,128]{1,0:T(8,128)(2,1)S(1)} %earlier_total.1), channel_id=1, source_target_pairs={{0,128},{8,136},{16,144},{24,152},{32,160},{40,168},{48,176},{56,1... | collective-permute-start | bytes 24584 | tf_op jit(solution)/shard_map/ppermute | solution.py:264
  56.6 18.0 %all-to-all-start.1 = ((bf16[16,32,128]{2,1,0:T(8,128)(2,1)}), bf16[16,32,128]{2,1,0:T(8,128)(2,1)S(1)}, u32[]{:S(2)}, u32[]{:S(2)}) async-start(bf16[16,32,128]{2,1,0:T(8,128)(2,1)} %earlier_carry.1), calls=%async_computation.1 | async-start | bytes 262144 | tf_op jit(solution)/shard_map/all_to_all | solution.py:256
  60.4 0.9 copy-start
  61.3 0.9 copy-start.2
  62.2 0.9 copy-start.4
  63.1 0.9 copy-start.5
  104.8 7.5 %collective-permute-start.5 = (bf16[32,128]{1,0:T(8,128)(2,1)S(1)}, bf16[32,128]{1,0:T(8,128)(2,1)S(1)}, u32[]{:S(2)}, u32[]{:S(2)}) collective-permute-start(bf16[32,128]{1,0:T(8,128)(2,1)S(1)} %later_total.1), channel_id=1, source_target_pairs={{384,0},{392,8},{400,16},{408,24},{416,32},{424,40},{432,48},{440,... | collective-permute-start | bytes 24584 | tf_op jit(solution)/shard_map/ppermute | solution.py:264
  108.3 4.1 %collective-permute-start.4 = (bf16[32,128]{1,0:T(8,128)(2,1)S(1)}, bf16[32,128]{1,0:T(8,128)(2,1)S(1)}, u32[]{:S(2)}, u32[]{:S(2)}) collective-permute-start(bf16[32,128]{1,0:T(8,128)(2,1)S(1)} %later_total.1), channel_id=1, source_target_pairs={{256,0},{264,8},{272,16},{280,24},{288,32},{296,40},{304,48},{312,... | collective-permute-start | bytes 24584 | tf_op jit(solution)/shard_map/ppermute | solution.py:264
  110.9 2.8 %collective-permute-start.3 = (bf16[32,128]{1,0:T(8,128)(2,1)S(1)}, bf16[32,128]{1,0:T(8,128)(2,1)S(1)}, u32[]{:S(2)}, u32[]{:S(2)}) collective-permute-start(bf16[32,128]{1,0:T(8,128)(2,1)S(1)} %later_total.1), channel_id=1, source_target_pairs={{128,0},{136,8},{144,16},{152,24},{160,32},{168,40},{176,48},{184,... | collective-permute-start | bytes 24584 | tf_op jit(solution)/shard_map/ppermute | solution.py:264
  114.4 19.1 %all-to-all-start.4 = ((bf16[16,32,128]{2,1,0:T(8,128)(2,1)}), bf16[16,32,128]{2,1,0:T(8,128)(2,1)S(1)}, u32[]{:S(2)}, u32[]{:S(2)}) async-start(bf16[16,32,128]{2,1,0:T(8,128)(2,1)} %later_carry.1), calls=%async_computation.4 | async-start | bytes 262144 | tf_op jit(solution)/shard_map/all_to_all | solution.py:256
  133.5 0.7 copy-start.6
Sparse Core Ops, SparseCore 0:
  23.9 86.3 all-gather.2

commit v4 on v3

--- a/solution.py
+++ b/solution.py
@@ -21,7 +21,7 @@
 CHUNK = 4
 
 BIG = 60 * 2**20
-COST = dict(own=1e8, local=1e8, total=1e5, carry=1e5, mix=1e8, norm=1e8, inside=1e8, final=1e8, soft=1e8)
+COST = dict(own=1e9, local=1e9, total=1e5, carry=1e5, mix=1e8, norm=1e8, inside=1e8, final=1e8, soft=1e8)
 
 epsilon = 1e-06
 floor_score = -1e30
@@ -42,7 +42,7 @@
     )
 
 
-def call(kernel, outs, *args, flops=1e8, name=None, vmem=16 * 2**20, scratch=(), smem=(), far=(), far_out=()):
+def call(kernel, outs, *args, flops=1e8, name=None, vmem=16 * 2**20, scratch=(), smem=(), far=(), far_out=(), smem_out=()):
     size = sum(a.size * a.dtype.itemsize for a in args)
     size += sum(math.prod(s) * jnp.dtype(d).itemsize for s, d in outs)
     specs = [
@@ -54,7 +54,9 @@
         out_shape=[jax.ShapeDtypeStruct(s, d) for s, d in outs],
         in_specs=specs,
         out_specs=[
-            pl.BlockSpec(memory_space=pltpu.HBM if i in far_out else pltpu.VMEM)
+            pl.BlockSpec(
+                memory_space=pltpu.HBM if i in far_out else pltpu.SMEM if i in smem_out else pltpu.VMEM
+            )
             for i in range(len(outs))
         ],
         scratch_shapes=list(scratch),
@@ -114,7 +116,8 @@
         local[:, h * HD : (h + 1) * HD] = dot(w, head(v, h), 1, 0)
 
 
-def total_kernel(r, tot):
+def total_kernel(r, after, tot):
+    del after
     acc = r[0].astype(f32)
     for i in range(1, NZ):
         acc = acc + r[i].astype(f32)
@@ -246,7 +249,7 @@
         return carry
 
     lax.fori_loop(first_chunk, my_chunk + 1, step, 0)
-    ended[...] = jnp.zeros((8, HD), f32)
+    ended[0] = my_chunk
     result = acc[...] / total[...]
     for h in range(HERE):
         out[:, h * HD : (h + 1) * HD] = jnp.transpose(result[:, h * T : (h + 1) * T]).astype(bf16)
@@ -256,10 +259,10 @@
     return lax.all_to_all(pieces, "ctx", 0, 0, tiled=True, axis_index_groups=z_groups)
 
 
-def carried_in(own, reverse):
+def carried_in(own, after, reverse):
     tag = "later" if reverse else "earlier"
     got = swap(own)
-    (line,) = call(total_kernel, [((PIECE, HD), bf16)], got, flops=COST["total"], name=tag + "_total")
+    (line,) = call(total_kernel, [((PIECE, HD), bf16)], got, after, flops=COST["total"], name=tag + "_total")
     sign = -1 if reverse else 1
     rows = [lax.ppermute(line, "ctx", y_shift(sign * s)) for s in (1, 2, 3)]
     (carried,) = call(
@@ -306,7 +309,7 @@
         scratch=[dma((2,))],
         flops=COST["local"], name="local",
     )
-    earlier = carried_in(own, False)
+    earlier = carried_in(own, local, False)
     mix, sums = call(
         mix_kernel, [(wide, f32), ((TP, 8, HD), f32)], q, g, local, earlier, flops=COST["mix"], name="mix"
     )
@@ -320,7 +323,6 @@
         sums,
         flops=COST["norm"], name="norm",
     )
-    later = carried_in(own_adjoint, True)
     grad_query, part_k, part_v = call(
         inside_kernel,
         [(wide, bf16), (wide, f32), (wide, f32)],
@@ -332,14 +334,16 @@
         earlier,
         flops=COST["inside"], name="inside",
     )
+    later = carried_in(own_adjoint, part_k, True)
     soft_out, ended = call(
         soft_kernel,
-        [(wide, bf16), ((8, HD), f32)],
+        [(wide, bf16), ((1,), jnp.int32)],
         soft_query,
         all_kv,
         doc_start.reshape(1, T),
         doc_start,
         smem=(3,),
+        smem_out=(1,),
         far=(0, 1),
         flops=COST["soft"],
         vmem=BIG,
@@ -356,7 +360,7 @@
         name="soft",
     )
     grad_key, grad_value = call(
-        final_kernel, [(wide, bf16), (wide, bf16)], k, v, part_k, part_v, later, ended, far=(5,), flops=COST["final"], name="final"
+        final_kernel, [(wide, bf16), (wide, bf16)], k, v, part_k, part_v, later, ended, smem=(5,), flops=COST["final"], name="final"
     )
     return (lin_out, grad_query, grad_key, grad_value, soft_out)
 

time: 144 us -> 143 us (level)
  blocking collectives: 67.2 us -> 41.6 us
  waiting for transfers between devices: 16.1 us -> 33.4 us
  starting transfers between devices: 20.5 us -> 30.6 us
  local copies, waits for them, and re-layouts: 4.31 us -> 1.82 us
    all_to_all x2 -> x1, blocking collectives: 43.4 us -> 17.7 us  [swap(): lax.all_to_all(pieces, 'ctx', 0, 0, tiled=True, axis_index_groups=z_groups)]
    all_to_all x2 -> x3, waiting for transfers between devices: 10.3 us -> 27.5 us  [swap(): lax.all_to_all(pieces, 'ctx', 0, 0, tiled=True, axis_index_groups=z_groups)]
    all_to_all x2 -> x3, starting transfers between devices: 9.1 us -> 19 us  [swap(): lax.all_to_all(pieces, 'ctx', 0, 0, tiled=True, axis_index_groups=z_groups)]
    unnamed x14 -> x12, local copies, waits for them, and re-layouts: 4.31 us -> 1.82 us
  transfers between devices with their start and end apart: 9 -> 10, of which waited for: 5 -> 6; matrix products, arithmetic and copies ran while one was open for 0% -> 0% of each run, Pallas kernels for 12% -> 11%
where the time goes in v4:
time: 143 us; the launch traced here: 141 us
  blocking collectives  41.6 us (29%)
  waiting for transfers between devices  33.4 us (23%)
  starting transfers between devices  30.6 us (21%)
  Pallas kernels  19.8 us (14%)
  between operations  14.2 us (10%)
  local copies, waits for them, and re-layouts  1.82 us (1%)
    all_to_all x3, waiting for transfers between devices, swap(): lax.all_to_all(pieces, 'ctx', 0, 0, tiled=True, axis_index_groups=z_groups)  27.5 us
    pallas_call x11, Pallas kernels, call(): pl.pallas_call(kernel, out_shape=[jax.ShapeDtypeStruct(s, d) for s, d in...  19.8 us
    all_to_all x3, starting transfers between devices, swap(): lax.all_to_all(pieces, 'ctx', 0, 0, tiled=True, axis_index_groups=z_groups)  19 us
    all_to_all x1, blocking collectives, swap(): lax.all_to_all(pieces, 'ctx', 0, 0, tiled=True, axis_index_groups=z_groups)  17.7 us
    all_to_all x1, blocking collectives, on_device(): lax.all_to_all(kv, 'ctx', 0, 0, tiled=True, axis_index_groups=y_groups)  14.4 us
    ppermute x6, starting transfers between devices, carried_in(): rows = [lax.ppermute(line, 'ctx', y_shift(sign * s)) for s in (1, 2, 3)]  11.6 us
    all_to_all x1, blocking collectives, on_device(): sums = lax.all_to_all(sums, 'tp', 0, 0, tiled=True)  9.49 us
    ppermute x6, waiting for transfers between devices, carried_in(): rows = [lax.ppermute(line, 'ctx', y_shift(sign * s)) for s in (1, 2, 3)]  5.78 us
  transfers between devices with their start and end apart: 10, of which 6 were waited for; matrix products, arithmetic and copies ran while one was open for 0% of the time, Pallas kernels for 11%

profile of v4, /device:TPU:24, one launch (start us, length us, event | category | flops | bytes accessed | tf_op | source)
XLA Modules:
  0.0 141.5 jit_solution(1549476395440995643)
XLA Ops:
  7.2 0.0 copy-start.5
  7.2 0.0 copy-start.4
  7.2 0.0 all-gather.3.cloned.1.call-start
  7.2 2.1 %own_state.1 = (bf16[16,32,128]{2,1,0:T(8,128)(2,1)}, bf16[4,2,128,128]{3,2,1,0:T(8,128)(2,1)}, bf16[128,512]{1,0:T(8,128)(2,1)}, bf16[128,512]{1,0:T(8,128)(2,1)}) custom-call(bf16[128,512]{1,0:T(8,128)(2,1)} %k_far.1, bf16[128,512]{1,0:T(8,128)(2,1)} %v_far.1, bf16[128,128]{1,0:T(8,128)(2,1)} %sk_far.1, bf16[128,128]{1,0:T(8,128)(2,1)} %sv_far.1), custom_call_target="tpu_custom_call" | custom-call | flops 1000000000 | bytes 983040 | tf_op jit(solution)/shard_map/own_state/pallas_call | solution.py:52
  9.3 0.0 copy-start.1
  9.4 0.0 copy-start.3
  9.4 14.4 %all_to_all.30 = bf16[4,2,128,128]{3,2,1,0:T(8,128)(2,1)} all-to-all(bf16[4,2,128,128]{3,2,1,0:T(8,128)(2,1)} %get-tuple-element.40), channel_id=1, replica_groups={{0,128,256,384},{8,136,264,392},{16,144,272,400},{24,152,280,408},{32,1..., dimensions={0} | all-to-all | bytes 524288 | tf_op jit(solution)/shard_map/all_to_all | solution.py:299
  23.8 0.0 all-gather.3.cloned.1.call-update
  23.8 10.3 %all-to-all-start = ((bf16[16,32,128]{2,1,0:T(8,128)(2,1)}), bf16[16,32,128]{2,1,0:T(8,128)(2,1)S(1)}, u32[]{:S(2)}, u32[]{:S(2)}) async-start(bf16[16,32,128]{2,1,0:T(8,128)(2,1)} %get-tuple-element.30), calls=%async_computation | async-start | bytes 262144 | tf_op jit(solution)/shard_map/all_to_all | solution.py:259
  34.2 0.0 copy-done.5
  34.2 0.0 copy-done.4
  34.2 0.0 copy-start
  34.2 0.9 copy-done
  35.1 0.0 copy-start.2
  35.1 0.9 copy-done.2
  36.0 1.1 local.1
  37.1 10.6 %all-to-all-done.r = bf16[16,32,128]{2,1,0:T(8,128)(2,1)S(1)} async-done(((bf16[16,32,128]{2,1,0:T(8,128)(2,1)}), bf16[16,32,128]{2,1,0:T(8,128)(2,1)S(1)}, u32[]{:S(2)}, u32[]{:S(2)}) %all-to-all-start) | async-done | bytes 131104 | tf_op jit(solution)/shard_map/all_to_all | solution.py:259
  47.6 1.3 collective-permute-start.2
  48.9 1.3 collective-permute-start.1
  50.2 1.3 collective-permute-start
  51.5 2.9 %collective-permute-done.2.c = bf16[32,128]{1,0:T(8,128)(2,1)S(1)} collective-permute-done((bf16[32,128]{1,0:T(8,128)(2,1)S(1)}, bf16[32,128]{1,0:T(8,128)(2,1)S(1)}, u32[]{:S(2)}, u32[]{:S(2)}) %collective-permute-start.2) | collective-permute-done | bytes 8224 | tf_op jit(solution)/shard_map/ppermute | solution.py:267
  54.4 1.6 %collective-permute-done.1.b = bf16[32,128]{1,0:T(8,128)(2,1)S(1)} collective-permute-done((bf16[32,128]{1,0:T(8,128)(2,1)S(1)}, bf16[32,128]{1,0:T(8,128)(2,1)S(1)}, u32[]{:S(2)}, u32[]{:S(2)}) %collective-permute-start.1) | collective-permute-done | bytes 8224 | tf_op jit(solution)/shard_map/ppermute | solution.py:267
  56.0 0.0 collective-permute-done.a
  56.0 17.7 %all_to_all.31.s = bf16[16,32,128]{2,1,0:T(8,128)(2,1)S(1)} all-to-all(bf16[16,32,128]{2,1,0:T(8,128)(2,1)S(1)} %earlier_carry.1), channel_id=1, replica_groups={{0,8,16,24,32,40,48,56,64,72,80,88,96,104,112,120},{128,136,144,152,160..., dimensions={0} | all-to-all | bytes 262144 | tf_op jit(solution)/shard_map/all_to_all | solution.py:259
  73.7 0.3 mix.1
  74.0 9.5 %all_to_all.32.sums = f32[8,8,128]{2,1,0:T(8,128)S(1)} all-to-all(f32[8,8,128]{2,1,0:T(8,128)S(1)} %get-tuple-element.32), channel_id=1, replica_groups=mesh['ctx'=64,'tp'=8] {'tp'}, dimensions={0} | all-to-all | bytes 65536 | tf_op jit(solution)/shard_map/all_to_all | solution.py:316
  83.5 1.1 norm.1
  84.6 4.4 %all-to-all-start.3 = ((bf16[16,32,128]{2,1,0:T(8,128)(2,1)}), bf16[16,32,128]{2,1,0:T(8,128)(2,1)S(1)}, u32[]{:S(2)}, u32[]{:S(2)}) async-start(bf16[16,32,128]{2,1,0:T(8,128)(2,1)} %get-tuple-element.39), calls=%async_computation.3 | async-start | bytes 262144 | tf_op jit(solution)/shard_map/all_to_all | solution.py:259
  89.0 0.0 copy-done.1
  89.0 0.0 copy-done.3
  89.0 1.4 inside.1
  90.4 14.7 %all-to-all-done.3.r = bf16[16,32,128]{2,1,0:T(8,128)(2,1)S(1)} async-done(((bf16[16,32,128]{2,1,0:T(8,128)(2,1)}), bf16[16,32,128]{2,1,0:T(8,128)(2,1)S(1)}, u32[]{:S(2)}, u32[]{:S(2)}) %all-to-all-start.3) | async-done | bytes 131104 | tf_op jit(solution)/shard_map/all_to_all | solution.py:259
  105.1 3.7 %collective-permute-start.5 = (bf16[32,128]{1,0:T(8,128)(2,1)S(1)}, bf16[32,128]{1,0:T(8,128)(2,1)S(1)}, u32[]{:S(2)}, u32[]{:S(2)}) collective-permute-start(bf16[32,128]{1,0:T(8,128)(2,1)S(1)} %later_total.1), channel_id=1, source_target_pairs={{384,0},{392,8},{400,16},{408,24},{416,32},{424,40},{432,48},{440,... | collective-permute-start | bytes 24584 | tf_op jit(solution)/shard_map/ppermute | solution.py:267
  108.8 1.7 %collective-permute-start.4 = (bf16[32,128]{1,0:T(8,128)(2,1)S(1)}, bf16[32,128]{1,0:T(8,128)(2,1)S(1)}, u32[]{:S(2)}, u32[]{:S(2)}) collective-permute-start(bf16[32,128]{1,0:T(8,128)(2,1)S(1)} %later_total.1), channel_id=1, source_target_pairs={{256,0},{264,8},{272,16},{280,24},{288,32},{296,40},{304,48},{312,... | collective-permute-start | bytes 24584 | tf_op jit(solution)/shard_map/ppermute | solution.py:267
  110.5 2.3 %collective-permute-start.3 = (bf16[32,128]{1,0:T(8,128)(2,1)S(1)}, bf16[32,128]{1,0:T(8,128)(2,1)S(1)}, u32[]{:S(2)}, u32[]{:S(2)}) collective-permute-start(bf16[32,128]{1,0:T(8,128)(2,1)S(1)} %later_total.1), channel_id=1, source_target_pairs={{128,0},{136,8},{144,16},{152,24},{160,32},{168,40},{176,48},{184,... | collective-permute-start | bytes 24584 | tf_op jit(solution)/shard_map/ppermute | solution.py:267
  112.9 0.0 collective-permute-done.5.c
  112.9 0.0 collective-permute-done.4.b
  112.9 1.3 collective-permute-done.3.a
  114.2 0.7 later_carry.1
  114.9 4.2 %all-to-all-start.4 = ((bf16[16,32,128]{2,1,0:T(8,128)(2,1)}), bf16[16,32,128]{2,1,0:T(8,128)(2,1)S(1)}, u32[]{:S(2)}, u32[]{:S(2)}) async-start(bf16[16,32,128]{2,1,0:T(8,128)(2,1)} %later_carry.1), calls=%async_computation.4 | async-start | bytes 262144 | tf_op jit(solution)/shard_map/all_to_all | solution.py:259
  119.2 0.0 all-gather.3.cloned.1.call-done
  119.2 11.6 %soft.1 = (bf16[128,512]{1,0:T(8,128)(2,1)}, s32[1]{0:T(128)}) custom-call(bf16[128,512]{1,0:T(8,128)(2,1)} %q_far.3, bf16[16,4,2,128,128]{4,3,2,1,0:T(8,128)(2,1)} %bitcast.2, s32[1,128]{1,0:T(1,128)} %bitcast.3, s32[128]{0:T(128)} %doc.1), custom_call_target="tpu_custom_call" | custom-call | flops 100000000 | bytes 4457476 | tf_op jit(solution)/shard_map/soft/pallas_call | solution.py:52
  130.8 2.3 %all-to-all-done.4.a = bf16[16,32,128]{2,1,0:T(8,128)(2,1)S(1)} async-done(((bf16[16,32,128]{2,1,0:T(8,128)(2,1)}), bf16[16,32,128]{2,1,0:T(8,128)(2,1)S(1)}, u32[]{:S(2)}, u32[]{:S(2)}) %all-to-all-start.4) | async-done | bytes 131104 | tf_op jit(solution)/shard_map/all_to_all | solution.py:259
  133.1 1.6 %final.1 = (bf16[128,512]{1,0:T(8,128)(2,1)}, bf16[128,512]{1,0:T(8,128)(2,1)}) custom-call(bf16[128,512]{1,0:T(8,128)(2,1)S(1)} %copy-done.1, bf16[128,512]{1,0:T(8,128)(2,1)S(1)} %copy-done.3, f32[128,512]{1,0:T(8,128)S(1)} %get-tuple-element.37.after.part_k, f32[128,512]{1,0:T(8,128)S(1)} %get-tuple-element.38.part_v, ...), custom_call_target="tpu_custom_call" | custom-call | flops 100000000 | bytes 1179652 | tf_op jit(solution)/shard_map/final/pallas_call | solution.py:52
  (3 shorter events, 0.1 us)
Async XLA Ops:
  7.2 27.0 %copy-start.5 = (bf16[128,512]{1,0:T(8,128)(2,1)S(1)}, bf16[128,512]{1,0:T(8,128)(2,1)}, u32[]{:S(2)}) copy-start(bf16[128,512]{1,0:T(8,128)(2,1)} %g_far.1) | copy-start | bytes 393220
  7.2 27.0 %copy-start.4 = (bf16[128,512]{1,0:T(8,128)(2,1)S(1)}, bf16[128,512]{1,0:T(8,128)(2,1)}, u32[]{:S(2)}) copy-start(bf16[128,512]{1,0:T(8,128)(2,1)} %q_far.2) | copy-start | bytes 393220
  7.2 112.0 %all-gather.3.cloned.1.call-start = ((), (), s32[]{:S(2)}) async-start(), calls=%async_computation.6 | async-start | bytes 4456448 | tf_op jit(solution)/shard_map/all_gather | solution.py:300
  9.3 79.7 %copy-start.1 = (bf16[128,512]{1,0:T(8,128)(2,1)S(1)}, bf16[128,512]{1,0:T(8,128)(2,1)}, u32[]{:S(2)}) copy-start(bf16[128,512]{1,0:T(8,128)(2,1)} %get-tuple-element.25.k) | copy-start | bytes 393220
  9.4 79.7 %copy-start.3 = (bf16[128,512]{1,0:T(8,128)(2,1)S(1)}, bf16[128,512]{1,0:T(8,128)(2,1)}, u32[]{:S(2)}) copy-start(bf16[128,512]{1,0:T(8,128)(2,1)} %get-tuple-element.26.v) | copy-start | bytes 393220
  23.8 23.8 %all-to-all-start = ((bf16[16,32,128]{2,1,0:T(8,128)(2,1)}), bf16[16,32,128]{2,1,0:T(8,128)(2,1)S(1)}, u32[]{:S(2)}, u32[]{:S(2)}) async-start(bf16[16,32,128]{2,1,0:T(8,128)(2,1)} %get-tuple-element.30), calls=%async_computation | async-start | bytes 262144 | tf_op jit(solution)/shard_map/all_to_all | solution.py:259
  34.2 0.9 copy-start
  35.1 0.9 copy-start.2
  47.6 6.8 %collective-permute-start.2 = (bf16[32,128]{1,0:T(8,128)(2,1)S(1)}, bf16[32,128]{1,0:T(8,128)(2,1)S(1)}, u32[]{:S(2)}, u32[]{:S(2)}) collective-permute-start(bf16[32,128]{1,0:T(8,128)(2,1)S(1)} %earlier_total.1), channel_id=1, source_target_pairs={{0,384},{8,392},{16,400},{24,408},{32,416},{40,424},{48,432},{56,4... | collective-permute-start | bytes 24584 | tf_op jit(solution)/shard_map/ppermute | solution.py:267
  48.9 7.0 %collective-permute-start.1 = (bf16[32,128]{1,0:T(8,128)(2,1)S(1)}, bf16[32,128]{1,0:T(8,128)(2,1)S(1)}, u32[]{:S(2)}, u32[]{:S(2)}) collective-permute-start(bf16[32,128]{1,0:T(8,128)(2,1)S(1)} %earlier_total.1), channel_id=1, source_target_pairs={{0,256},{8,264},{16,272},{24,280},{32,288},{40,296},{48,304},{56,3... | collective-permute-start | bytes 24584 | tf_op jit(solution)/shard_map/ppermute | solution.py:267
  50.2 5.8 %collective-permute-start = (bf16[32,128]{1,0:T(8,128)(2,1)S(1)}, bf16[32,128]{1,0:T(8,128)(2,1)S(1)}, u32[]{:S(2)}, u32[]{:S(2)}) collective-permute-start(bf16[32,128]{1,0:T(8,128)(2,1)S(1)} %earlier_total.1), channel_id=1, source_target_pairs={{0,128},{8,136},{16,144},{24,152},{32,160},{40,168},{48,176},{56,1... | collective-permute-start | bytes 24584 | tf_op jit(solution)/shard_map/ppermute | solution.py:267
  84.6 20.5 %all-to-all-start.3 = ((bf16[16,32,128]{2,1,0:T(8,128)(2,1)}), bf16[16,32,128]{2,1,0:T(8,128)(2,1)S(1)}, u32[]{:S(2)}, u32[]{:S(2)}) async-start(bf16[16,32,128]{2,1,0:T(8,128)(2,1)} %get-tuple-element.39), calls=%async_computation.3 | async-start | bytes 262144 | tf_op jit(solution)/shard_map/all_to_all | solution.py:259
  105.1 7.7 %collective-permute-start.5 = (bf16[32,128]{1,0:T(8,128)(2,1)S(1)}, bf16[32,128]{1,0:T(8,128)(2,1)S(1)}, u32[]{:S(2)}, u32[]{:S(2)}) collective-permute-start(bf16[32,128]{1,0:T(8,128)(2,1)S(1)} %later_total.1), channel_id=1, source_target_pairs={{384,0},{392,8},{400,16},{408,24},{416,32},{424,40},{432,48},{440,... | collective-permute-start | bytes 24584 | tf_op jit(solution)/shard_map/ppermute | solution.py:267
  108.8 4.1 %collective-permute-start.4 = (bf16[32,128]{1,0:T(8,128)(2,1)S(1)}, bf16[32,128]{1,0:T(8,128)(2,1)S(1)}, u32[]{:S(2)}, u32[]{:S(2)}) collective-permute-start(bf16[32,128]{1,0:T(8,128)(2,1)S(1)} %later_total.1), channel_id=1, source_target_pairs={{256,0},{264,8},{272,16},{280,24},{288,32},{296,40},{304,48},{312,... | collective-permute-start | bytes 24584 | tf_op jit(solution)/shard_map/ppermute | solution.py:267
  110.5 3.7 %collective-permute-start.3 = (bf16[32,128]{1,0:T(8,128)(2,1)S(1)}, bf16[32,128]{1,0:T(8,128)(2,1)S(1)}, u32[]{:S(2)}, u32[]{:S(2)}) collective-permute-start(bf16[32,128]{1,0:T(8,128)(2,1)S(1)} %later_total.1), channel_id=1, source_target_pairs={{128,0},{136,8},{144,16},{152,24},{160,32},{168,40},{176,48},{184,... | collective-permute-start | bytes 24584 | tf_op jit(solution)/shard_map/ppermute | solution.py:267
  114.9 18.1 %all-to-all-start.4 = ((bf16[16,32,128]{2,1,0:T(8,128)(2,1)}), bf16[16,32,128]{2,1,0:T(8,128)(2,1)S(1)}, u32[]{:S(2)}, u32[]{:S(2)}) async-start(bf16[16,32,128]{2,1,0:T(8,128)(2,1)} %later_carry.1), calls=%async_computation.4 | async-start | bytes 262144 | tf_op jit(solution)/shard_map/all_to_all | solution.py:259
Sparse Core Ops, SparseCore 0:
  24.0 86.0 all-gather.2
